TPU v7x, 32 devices: a whole 2x2x4 slice. The times are simulated.
32 devices in a mesh: dp: 8 (over z, x), mp: 4 (over y, core).
Axes of the slice: x: 2, y: 2, z: 4, core: 2. Of those that a mesh axis runs over, the one named last changes fastest.
Arguments:
- input_steps: bfloat16 [4, 768, 8192], P(None, 'dp', 'mp'), may hold values from -6 to 6
- gate_steps: bfloat16 [4, 768, 8192], P(None, 'dp', 'mp'), may hold values from -6 to 6
- conv_state: bfloat16 [768, 3, 8192], P('dp', None, 'mp'), may hold values from -6 to 6
- ssm_state: bfloat16 [768, 16, 8192], P('dp', None, 'mp'), may hold values from -6 to 6
- new_slot: int32 [768], replicated, may hold values from 0 to 767, as said below
- remaining: int32 [768], replicated, may hold values from 1 to 4
- conv_weight: float32 [4, 8192], P(None, 'mp'), may hold values from -3 to 3
- conv_bias: float32 [8192], P('mp'), may hold values from -3 to 3
- coef_proj: bfloat16 [8192, 544], P('mp', 'dp'), may hold values from -0.0625 to 0.0625
- delta_proj: bfloat16 [512, 8192], P('dp', 'mp'), may hold values from -0.25 to 0.25
- delta_bias: float32 [8192], P('mp'), may hold values from -4 to -1
- decay_log: float32 [16, 8192], P(None, 'mp'), may hold values from -1 to 2
- skip_gain: float32 [8192], P('mp'), may hold values from 0.5 to 1.5
- out_proj: bfloat16 [8192, 4096], P('mp', 'dp'), may hold values from -0.0625 to 0.0625
Outputs:
- layer_out: bfloat16 [4, 768, 4096], P(None, 'dp', 'mp')
- conv_final: bfloat16 [768, 3, 8192], P('dp', None, 'mp')
- ssm_final: bfloat16 [768, 16, 8192], P('dp', None, 'mp')
Inputs may be any that keep to these rules, and one draw needn't show every extreme that they name: new_slot is a permutation of the rollouts. Each group hands to every group 0, 12 or 24 of its rollouts: 24 to exactly one group and 0 to exactly one group; each group receives 24 from exactly one group and 0 from exactly one group.
All inputs are finite; a program needn't handle non-finite values.
Results may differ from a plain program's by a relative error of at most 0.03.
Values may be sent and summed in bfloat16 or wider, within the bound.
A program may use at most 128 MiB of HBM per device.

v0:
```python
import jax
import jax.numpy as jnp
from jax import lax
from jax.sharding import PartitionSpec as P


def per_device(
    input_steps,
    gate_steps,
    conv_state,
    ssm_state,
    new_slot,
    remaining,
    conv_weight,
    conv_bias,
    coef_proj,
    delta_proj,
    delta_bias,
    decay_log,
    skip_gain,
    out_proj,
):
    groups = lax.axis_size("dp")
    my_group = lax.axis_index("dp")
    row_count = conv_state.shape[0]
    channels = conv_state.shape[2]
    state_len = ssm_state.shape[1]
    steps_total = input_steps.shape[0]
    capacity = 2 * row_count // groups
    total_rows = new_slot.shape[0]
    target = new_slot // row_count
    group_ids = jnp.arange(groups, dtype=jnp.int32)
    marks = (target[:, None] == group_ids[None, :]).astype(jnp.int32)
    ranks = (
        jnp.cumsum(marks.reshape(groups, row_count, groups), axis=1).reshape(total_rows, groups) - 1
    )
    placed = jnp.sum(ranks * marks, axis=1)
    source = jnp.arange(total_rows, dtype=jnp.int32) // row_count
    inverse = (
        jnp.zeros((total_rows,), jnp.int32)
        .at[new_slot]
        .set(jnp.arange(total_rows, dtype=jnp.int32))
    )
    anchor = lax.dynamic_slice_in_dim(inverse, my_group * row_count, row_count)
    remain_new = remaining[anchor]
    my_target = lax.dynamic_slice_in_dim(target, my_group * row_count, row_count)
    my_placed = lax.dynamic_slice_in_dim(placed, my_group * row_count, row_count)
    from_group = source[anchor]
    from_rank = placed[anchor]

    def relocate(state):
        depth = state.shape[1]
        send_index = my_target * capacity + my_placed
        buffer = (
            jnp.zeros((groups * capacity, depth, channels), state.dtype).at[send_index].set(state)
        )
        moved = lax.all_to_all(buffer, "dp", split_axis=0, concat_axis=0, tiled=True)
        return moved[from_group * capacity + from_rank]

    coef_whole = lax.all_gather(coef_proj, "dp", axis=1, tiled=True)
    delta_whole = lax.all_gather(delta_proj, "dp", axis=0, tiled=True)
    rank_len = delta_whole.shape[0]
    decay_rate = -jnp.exp(decay_log)
    outputs = []
    window = relocate(conv_state).astype(jnp.float32)
    hidden = relocate(ssm_state).astype(jnp.float32)
    for position in range(steps_total):
        active = (remain_new > position)[:, None]
        full_window = jnp.concatenate(
            [window, input_steps[position].astype(jnp.float32)[:, None, :]], axis=1
        )
        conv_out = jnp.sum(full_window * conv_weight[None], axis=1) + conv_bias
        full_window, activated = (full_window, jax.nn.silu(conv_out))
        partial_value = jnp.dot(
            activated.astype(jnp.bfloat16), coef_whole, preferred_element_type=jnp.float32
        )
        low_rank = lax.psum(partial_value.astype(jnp.bfloat16), "mp").astype(jnp.float32)
        step_in = low_rank[:, :rank_len].astype(jnp.bfloat16)
        input_coef = low_rank[:, rank_len : rank_len + state_len]
        output_coef = low_rank[:, rank_len + state_len :]
        step_size = jax.nn.softplus(
            jnp.dot(step_in, delta_whole, preferred_element_type=jnp.float32) + delta_bias
        )
        step_size, input_coef, output_coef = (step_size, input_coef, output_coef)
        decay_factor = jnp.exp(step_size[:, None, :] * decay_rate[None])
        updated = (
            decay_factor * hidden + (step_size * activated)[:, None, :] * input_coef[:, :, None]
        )
        mixer = (
            jnp.sum(updated * output_coef[:, :, None], axis=1) + skip_gain * activated
        ) * jax.nn.silu(gate_steps[position].astype(jnp.float32))
        hidden = jnp.where(active[:, :, None], updated, hidden)
        window = jnp.where(active[:, :, None], full_window[:, 1:], window)
        outputs.append(jnp.where(active, mixer, 0.0).astype(jnp.bfloat16))
    stacked = jnp.stack(outputs).reshape(steps_total * row_count, channels)
    partial_mix = jnp.dot(
        stacked,
        lax.all_gather(out_proj, "dp", axis=1, tiled=True),
        preferred_element_type=jnp.float32,
    )
    summed = lax.psum_scatter(
        partial_mix.astype(jnp.bfloat16), "mp", scatter_dimension=1, tiled=True
    )
    layer_out = summed.reshape(steps_total, row_count, summed.shape[1])
    return (layer_out, window.astype(jnp.bfloat16), hidden.astype(jnp.bfloat16))


def solution(mesh):
    return jax.shard_map(
        per_device,
        mesh=mesh,
        in_specs=(
            P(None, "dp", "mp"),
            P(None, "dp", "mp"),
            P("dp", None, "mp"),
            P("dp", None, "mp"),
            P(),
            P(),
            P(None, "mp"),
            P("mp"),
            P("mp", "dp"),
            P("dp", "mp"),
            P("mp"),
            P(None, "mp"),
            P("mp"),
            P("mp", "dp"),
        ),
        out_specs=(P(None, "dp", "mp"), P("dp", None, "mp"), P("dp", None, "mp")),
        check_vma=False,
    )
```

profile of v0, /device:TPU:0, one launch (start us, length us, event | category | flops | bytes accessed | tf_op | source)
XLA Modules:
  0.0 786.1 jit_solution(7591653813472761899)
XLA Ops:
  12.4 3.4 scatter_custom_fusion
  15.9 3.3 broadcast_in_dim.143
  19.1 12.0 %scatter_fusion = bf16[192,3,2048]{2,1,0:T(4,128)(2,1)} fusion(bf16[192,3,2048]{2,1,0:T(4,128)(2,1)} %broadcast_in_dim.143, s32[96]{0:T(128)S(1)} %get-tuple-element.55, bf16[96,3,2048]{2,1,0:T(4,128)(2,1)S(1)} %copy.33), kind=kCustom, calls=%fused_computation.6 | custom fusion | bytes 3539328 | tf_op jit(solution)/shard_map/scatter | solution.py:55
  31.1 7.3 all-to-all-start
  48.0 83.8 %all-gather.9.cloned.1.call-done = bf16[8,68,2048]{2,1,0:T(8,128)(2,1)} async-done(((bf16[1,68,2048]{2,1,0:T(8,128)(2,1)}), bf16[8,68,2048]{2,1,0:T(8,128)(2,1)}) %all-gather.9.cloned.1.call-update) | async-done | bytes 2228240 | tf_op jit(solution)/shard_map/all_gather | solution.py:60
  131.8 4.1 reshape.544
  137.6 3.8 gather_fusion.3
  148.9 12.8 %fusion.17 = (f32[96,2048]{1,0:T(8,128)S(1)}, f32[96,2048]{1,0:T(8,128)S(1)}, f32[96,2048]{1,0:T(8,128)S(1)}, f32[96,2048]{1,0:T(8,128)S(1)}) fusion(f32[96,1,2048]{2,1,0:T(1,128)S(1)} %copy-done.5, f32[96,3,2048]{2,1,0:T(4,128)S(1)} %convert_element_type.144, f32[4,2048]{1,0:T(4,128)S(1)} %copy-done.32, f32[96,1,2048]{2,1,0:T(1,128)S(1)} %copy-done.3, ...), kind=kLoop, calls=%fused_computation.44 | loop fusion | flops 8650752 | bytes 15761408 | tf_op jit(solution)/shard_map/reduce_sum | solution.py:72
  169.4 6.2 broadcast_in_dim.145
  175.6 17.9 %scatter_fusion.1 = bf16[192,16,2048]{2,1,0:T(8,128)(2,1)} fusion(bf16[192,16,2048]{2,1,0:T(8,128)(2,1)} %broadcast_in_dim.145, s32[96]{0:T(128)S(1)} %get-tuple-element.55, bf16[96,16,2048]{2,1,0:T(8,128)(2,1)} %param.17), kind=kCustom, calls=%fused_computation.7 | custom fusion | bytes 18874752 | tf_op jit(solution)/shard_map/scatter | solution.py:55
  193.5 5.5 all-to-all-start.1
  206.6 232.4 %all-gather.5.cloned.1.call-done = bf16[512,2048]{1,0:T(8,128)(2,1)} async-done(((bf16[64,2048]{1,0:T(8,128)(2,1)}), bf16[512,2048]{1,0:T(8,128)(2,1)}) %all-gather.5.cloned.1.call-update) | async-done | bytes 2097168 | tf_op jit(solution)/shard_map/all_gather | solution.py:61
  441.6 2.7 compare_select_fusion.2
  446.2 3.0 fusion.62
  449.2 103.4 %all-to-all-done.1 = bf16[192,16,2048]{2,1,0:T(8,128)(2,1)} async-done(((bf16[192,16,2048]{2,1,0:T(8,128)(2,1)}), bf16[192,16,2048]{2,1,0:T(8,128)(2,1)}, u32[]{:S(2)}, u32[]{:S(2)}) %all-to-all-start.1) | async-done | bytes 12582944 | tf_op jit(solution)/shard_map/all_to_all | solution.py:57
  552.6 11.0 %gather_fusion.4 = bf16[96,16,2048]{2,1,0:T(8,128)(2,1)} fusion(bf16[192,16,2048]{2,1,0:T(8,128)(2,1)} %all-to-all-done.1, s32[1024]{0:T(1024)} %copy-done.36), kind=kCustom, calls=%fused_computation.4 | custom fusion | bytes 12583296 | tf_op jit(solution)/shard_map/gather | solution.py:58
  563.7 18.2 %multiply_reduce_fusion.3 = (f32[96,2048]{1,0:T(8,128)}, f32[96,2048]{1,0:T(8,128)}) fusion(bf16[96,16,2048]{2,1,0:T(8,128)(2,1)} %gather_fusion.4, f32[96,16]{1,0:T(8,128)S(1)} %copy-done.30, f32[96,16]{1,0:T(8,128)S(1)} %copy-done.25, f32[96,2048]{1,0:T(8,128)} %get-tuple-element.43, f32[16,2048]{1,0:T(8,128)S(1)} %exponential_negate_fusion, ...), kind=kLoop, calls=%fused_computation.20 | loop fusion | flops 43646976 | bytes 11165792 | tf_op jit(solution)/shard_map/reduce_sum | solution.py:90
  582.0 23.9 %multiply_reduce_fusion.1 = (f32[96,2048]{1,0:T(8,128)}, f32[96,2048]{1,0:T(8,128)}) fusion(f32[96,16]{1,0:T(8,128)S(1)} %copy-done.29, f32[96,16]{1,0:T(8,128)S(1)} %copy-done.27, f32[96,2048]{1,0:T(8,128)} %get-tuple-element.41, f32[96,2048]{1,0:T(8,128)} %copy-done.46, f32[16,2048]{1,0:T(8,128)S(1)} %exponential_negate_fusion, ...), kind=kLoop, calls=%fused_computation.14 | loop fusion | flops 75104256 | bytes 14324000 | tf_op jit(solution)/shard_map/reduce_sum | solution.py:90
  606.0 3.5 fusion.47
  610.8 120.1 %all-gather.7.cloned.1.call-done = bf16[2048,4096]{1,0:T(8,128)(2,1)} async-done(((bf16[2048,512]{1,0:T(8,128)(2,1)}), bf16[2048,4096]{1,0:T(8,128)(2,1)}) %all-gather.7.cloned.1.call-update) | async-done | bytes 16777232 | tf_op jit(solution)/shard_map/all_gather | solution.py:98
  730.9 11.9 %convolution_convert_fusion = bf16[384,4096]{1,0:T(8,128)(2,1)} fusion(bf16[384,2048]{1,0:T(8,128)(2,1)} %bitcast.89, bf16[2048,4096]{1,0:T(8,128)(2,1)} %all-gather.7.cloned.1.call-done), kind=kOutput, calls=%fused_computation.21 | convolution fusion | flops 6444023808 | bytes 21495808 | tf_op jit(solution)/shard_map/dot_general | solution.py:96
  742.9 3.7 fusion.7
  748.5 19.9 %select_convert_fusion = bf16[96,16,2048]{2,1,0:T(8,128)(2,1)} fusion(f32[96,16]{1,0:T(8,128)S(1)} %copy-done.28, f32[96,2048]{1,0:T(8,128)S(1)} %copy-done.54, f32[96,2048]{1,0:T(8,128)S(1)} %copy-done.56, f32[96,16]{1,0:T(8,128)S(1)} %copy-done.27, f32[96,2048]{1,0:T(8,128)S(1)} %copy-done.55, f32[96,2048]{1,0:T(8,128)S(1)} %copy-done.47, ...), kind=kLoop, calls=%fused_computation.11 | loop fusion | flops 69206016 | bytes 19030400 | tf_op jit(solution)/shard_map/convert_element_type | solution.py:105
  768.4 10.7 %reduce-scatter.2.cloned.1.call-done = bf16[384,1024]{1,0:T(8,128)(2,1)} async-done(((bf16[384,4096]{1,0:T(8,128)(2,1)}), bf16[384,1024]{1,0:T(8,128)(2,1)}) %reduce-scatter.2.cloned.1.call-update) | async-done | bytes 786448 | tf_op jit(solution)/shard_map/reduce_scatter | solution.py:101
  (168 shorter events, 46.8 us)
Async XLA Ops:
  7.2 34.1 %copy-start = (s32[768]{0:T(1024)S(1)}, s32[768]{0:T(1024)}, u32[]{:S(2)}) copy-start(s32[768]{0:T(1024)} %param.19) | copy-start | bytes 9220
  31.1 106.5 %all-to-all-start = ((bf16[192,3,2048]{2,1,0:T(4,128)(2,1)}), bf16[192,3,2048]{2,1,0:T(4,128)(2,1)}, u32[]{:S(2)}, u32[]{:S(2)}) async-start(bf16[192,3,2048]{2,1,0:T(4,128)(2,1)} %scatter_fusion), calls=%async_computation | async-start | bytes 6291456 | tf_op jit(solution)/shard_map/all_to_all | solution.py:57
  38.4 93.5 %all-gather.9.cloned.1.call-start = ((), (), s32[]{:S(2)}) async-start(), calls=%async_computation.6 | async-start | bytes 2654208 | tf_op jit(solution)/shard_map/all_gather | solution.py:60
  39.1 161.4 %all-reduce.3.cloned.1.call-start = ((), (), s32[]{:S(2)}) async-start(), calls=%async_computation.7 | async-start | bytes 983040 | tf_op jit(solution)/shard_map/psum | solution.py:77
  42.3 99.1 %copy-start.36 = (s32[1024]{0:T(1024)}, s32[1024]{0:T(1024)S(1)}, u32[]{:S(2)}) copy-start(s32[1024]{0:T(1024)S(1)} %pad_clamp_fusion) | copy-start | bytes 12292
  42.9 99.0 %copy-start.42 = (pred[96]{0:T(512)(128)(4,1)}, pred[96]{0:T(512)(128)(4,1)S(1)}, u32[]{:S(2)}) copy-start(pred[96]{0:T(512)(128)(4,1)S(1)} %get-tuple-element.49) | copy-start | bytes 292
  42.9 101.3 %copy-start.40 = (pred[96]{0:T(512)(128)(4,1)}, pred[96]{0:T(512)(128)(4,1)S(1)}, u32[]{:S(2)}) copy-start(pred[96]{0:T(512)(128)(4,1)S(1)} %get-tuple-element.48) | copy-start | bytes 292
  42.9 103.7 %copy-start.38 = (pred[96]{0:T(512)(128)(4,1)}, pred[96]{0:T(512)(128)(4,1)S(1)}, u32[]{:S(2)}) copy-start(pred[96]{0:T(512)(128)(4,1)S(1)} %get-tuple-element.47) | copy-start | bytes 292
  45.6 96.3 %copy-start.4 = (f32[96,1,2048]{2,1,0:T(1,128)}, f32[96,1,2048]{2,1,0:T(1,128)S(1)}, u32[]{:S(2)}) copy-start(f32[96,1,2048]{2,1,0:T(1,128)S(1)} %get-tuple-element.54) | copy-start | bytes 2359300
  45.6 98.6 %copy-start.2 = (f32[96,1,2048]{2,1,0:T(1,128)}, f32[96,1,2048]{2,1,0:T(1,128)S(1)}, u32[]{:S(2)}) copy-start(f32[96,1,2048]{2,1,0:T(1,128)S(1)} %get-tuple-element.53) | copy-start | bytes 2359300
  168.1 271.0 %all-gather.5.cloned.1.call-start = ((), (), s32[]{:S(2)}) async-start(), calls=%async_computation.3 | async-start | bytes 2359296 | tf_op jit(solution)/shard_map/all_gather | solution.py:61
  168.8 562.1 %all-gather.7.cloned.1.call-start = ((), (), s32[]{:S(2)}) async-start(), calls=%async_computation.4 | async-start | bytes 18874368 | tf_op jit(solution)/shard_map/all_gather | solution.py:98
  193.5 245.6 %copy-start.45 = (f32[2048]{0:T(1024)S(1)}, f32[2048]{0:T(1024)}, u32[]{:S(2)}) copy-start(f32[2048]{0:T(1024)} %param.24) | copy-start | bytes 24580
  193.5 359.1 %all-to-all-start.1 = ((bf16[192,16,2048]{2,1,0:T(8,128)(2,1)}), bf16[192,16,2048]{2,1,0:T(8,128)(2,1)}, u32[]{:S(2)}, u32[]{:S(2)}) async-start(bf16[192,16,2048]{2,1,0:T(8,128)(2,1)} %scatter_fusion.1), calls=%async_computation.1 | async-start | bytes 25165824 | tf_op jit(solution)/shard_map/all_to_all | solution.py:57
  199.0 580.1 %reduce-scatter.2.cloned.1.call-start = ((), (), s32[]{:S(2)}) async-start(), calls=%async_computation.5 | async-start | bytes 3932160 | tf_op jit(solution)/shard_map/reduce_scatter | solution.py:101
  200.5 243.8 %copy-start.24 = (bf16[96,544]{1,0:T(8,128)(2,1)S(1)}, bf16[96,544]{1,0:T(8,128)(2,1)}, u32[]{:S(2)}) copy-start(bf16[96,544]{1,0:T(8,128)(2,1)} %get-tuple-element.20) | copy-start | bytes 313348
  200.5 245.6 %copy-start.23 = (bf16[96,544]{1,0:T(8,128)(2,1)S(1)}, bf16[96,544]{1,0:T(8,128)(2,1)}, u32[]{:S(2)}) copy-start(bf16[96,544]{1,0:T(8,128)(2,1)} %get-tuple-element.23) | copy-start | bytes 313348
  449.1 114.5 %copy-start.25 = (f32[96,16]{1,0:T(8,128)S(1)}, f32[96,16]{1,0:T(8,128)}, u32[]{:S(2)}) copy-start(f32[96,16]{1,0:T(8,128)} %get-tuple-element.35) | copy-start | bytes 18436
  449.1 114.5 %copy-start.26 = (f32[96,16]{1,0:T(8,128)S(1)}, f32[96,16]{1,0:T(8,128)}, u32[]{:S(2)}) copy-start(f32[96,16]{1,0:T(8,128)} %get-tuple-element.33) | copy-start | bytes 18436
  449.2 114.5 %copy-start.30 = (f32[96,16]{1,0:T(8,128)S(1)}, f32[96,16]{1,0:T(8,128)}, u32[]{:S(2)}) copy-start(f32[96,16]{1,0:T(8,128)} %get-tuple-element.34) | copy-start | bytes 18436
  449.2 114.5 %copy-start.43 = (pred[96]{0:T(512)(128)(4,1)S(1)}, pred[96]{0:T(512)(128)(4,1)}, u32[]{:S(2)}) copy-start(pred[96]{0:T(512)(128)(4,1)} %copy-done.42) | copy-start | bytes 292
  581.9 24.0 %copy-start.10 = (f32[96,2048]{1,0:T(8,128)S(1)}, f32[96,2048]{1,0:T(8,128)}, u32[]{:S(2)}) copy-start(f32[96,2048]{1,0:T(8,128)} %copy-done.8) | copy-start | bytes 2359300
  581.9 24.0 %copy-start.13 = (f32[96,2048]{1,0:T(8,128)S(1)}, f32[96,2048]{1,0:T(8,128)}, u32[]{:S(2)}) copy-start(f32[96,2048]{1,0:T(8,128)} %copy-done.11) | copy-start | bytes 2359300
  746.6 32.5 %copy-start.1 = (s32[768]{0:T(1024)S(1)}, s32[768]{0:T(1024)}, u32[]{:S(2)}) copy-start(s32[768]{0:T(1024)} %param.19) | copy-start | bytes 9220
  (42 other events, 445.2 us)
Sparse Core Ops, SparseCore 0:
  41.4 90.3 all-gather.8
  168.2 32.3 all-reduce.2
  202.9 236.1 all-gather.4
  441.1 289.7 all-gather.6
  742.9 36.1 reduce-scatter.1
where the time goes:
time: 792 us; the launch traced here: 786 us
  waiting for transfers between devices  556 us (70%)
  other arithmetic  97.4 us (12%)
  local copies, waits for them, and re-layouts  77.8 us (10%)
  matrix products  27.1 us (3%)
  between operations  15.1 us (2%)
  starting transfers between devices  13.1 us (2%)
    all_gather x1, waiting for transfers between devices, per_device(): delta_whole = lax.all_gather(delta_proj, 'dp', axis=0, tiled=True)  232 us
    all_gather x1, waiting for transfers between devices, per_device(): lax.all_gather(out_proj, 'dp', axis=1, tiled=True)  120 us
    all_to_all x2, waiting for transfers between devices, relocate(): lax.all_to_all(buffer, 'dp', split_axis=0, concat_axis=0, tiled=True)  105 us
    all_gather x1, waiting for transfers between devices, per_device(): coef_whole = lax.all_gather(coef_proj, 'dp', axis=1, tiled=True)  83.8 us
    reduce_sum x2, other arithmetic, per_device(): jnp.sum(updated * output_coef[:, :, None], axis=1) + skip_gain * activated  42.1 us
    scatter x2, local copies, waits for them, and re-layouts, relocate(): jnp.zeros((groups * capacity, depth, channels), state.dtype).at[send_index]  29.8 us
    convert_element_type x2, other arithmetic, per_device(): return (layer_out, window.astype(jnp.bfloat16), hidden.astype(jnp.bfloat16))  23.5 us
  transfers between devices with their start and end apart: 7, of which 7 were waited for; matrix products, arithmetic and copies ran while one was open for 17% of the time, Pallas kernels for 0%

commit v1 on v0

v1 whole, which is shorter than its diff:
```python
import jax
import jax.numpy as jnp
from jax import lax
from jax.experimental import pallas as pl
from jax.experimental.pallas import tpu as pltpu
from jax.sharding import PartitionSpec as P

VMEM_LIMIT = 48 * 1024 * 1024


def pack_kernel(index_ref, state_ref, base_ref, extra_ref):
    block = pl.program_id(0)
    cap = base_ref.shape[0]
    blocks = pl.num_programs(0)
    for i in range(cap):
        base_ref[i] = state_ref[index_ref[block * cap + i]]

    @pl.when(block == 0)
    def _():
        for i in range(cap):
            extra_ref[i] = state_ref[index_ref[blocks * cap + i]]


def pack(index, state, groups):
    rows, depth, channels = state.shape
    cap = rows // groups
    return pl.pallas_call(
        pack_kernel,
        out_shape=(
            jax.ShapeDtypeStruct((rows, depth, channels), state.dtype),
            jax.ShapeDtypeStruct((cap, depth, channels), state.dtype),
        ),
        grid_spec=pltpu.PrefetchScalarGridSpec(
            num_scalar_prefetch=1,
            grid=(groups,),
            in_specs=[
                pl.BlockSpec((rows, depth, channels), lambda i, _: (0, 0, 0)),
            ],
            out_specs=(
                pl.BlockSpec((cap, depth, channels), lambda i, _: (i, 0, 0)),
                pl.BlockSpec((cap, depth, channels), lambda i, _: (0, 0, 0)),
            ),
        ),
        compiler_params=pltpu.CompilerParams(vmem_limit_bytes=VMEM_LIMIT),
        cost_estimate=pl.CostEstimate(
            flops=0, bytes_accessed=4 * state.size, transcendentals=0
        ),
    )(index, state)


def scan_kernel(
    slot_ref,
    base_ref,
    extra_ref,
    step_ref,
    act_ref,
    gate_ref,
    coef_ref,
    mask_ref,
    decay_ref,
    skip_ref,
    mix_ref,
    final_ref,
    read_ref,
):
    first = pl.program_id(0) * step_ref.shape[1]
    rows_total = base_ref.shape[0]
    steps, rows, channels = step_ref.shape
    width = min(512, channels)

    def one_row(r, carry):
        slot = slot_ref[first + r]
        in_base = slot < rows_total
        at_base = jnp.minimum(slot, rows_total - 1)
        at_extra = jnp.maximum(slot - rows_total, 0)
        coef = coef_ref[r]
        for c in range(0, channels, width):
            cols = pl.ds(c, width)
            hidden = jnp.where(
                in_base,
                base_ref[at_base, :, cols].astype(jnp.float32),
                extra_ref[at_extra, :, cols].astype(jnp.float32),
            )
            decay = decay_ref[:, cols]
            for t in range(steps):
                step = step_ref[t, pl.ds(r, 1), cols]
                act = act_ref[t, pl.ds(r, 1), cols]
                hidden = (
                    jnp.exp(step * decay) * hidden + (step * act) * coef[:, 2 * t : 2 * t + 1]
                )
                read_ref[t, pl.ds(r, 1), cols] = jnp.sum(
                    hidden * coef[:, 2 * t + 1 : 2 * t + 2], axis=0, keepdims=True
                )
            final_ref[r, :, cols] = hidden.astype(final_ref.dtype)
        return carry

    lax.fori_loop(0, rows, one_row, 0)
    for t in range(steps):
        gate = gate_ref[t].astype(jnp.float32)
        mixer = (read_ref[t] + skip_ref[...] * act_ref[t]) * jax.nn.silu(gate)
        mix_ref[t] = jnp.where(mask_ref[:, t : t + 1] > 0, mixer, 0.0).astype(mix_ref.dtype)


def scan(slot, base, extra, step, act, gate, coef, mask, decay, skip):
    rows, depth, channels = base.shape
    steps = step.shape[0]
    tile = 16
    cap = extra.shape[0]

    def whole(shape):
        return pl.BlockSpec(shape, lambda i, _: (0,) * len(shape))

    per_step = pl.BlockSpec((steps, tile, channels), lambda i, _: (0, i, 0))
    return pl.pallas_call(
        scan_kernel,
        out_shape=(
            jax.ShapeDtypeStruct((steps, rows, channels), jnp.bfloat16),
            jax.ShapeDtypeStruct((rows, depth, channels), jnp.bfloat16),
        ),
        grid_spec=pltpu.PrefetchScalarGridSpec(
            num_scalar_prefetch=1,
            grid=(rows // tile,),
            in_specs=[
                whole((rows, depth, channels)),
                whole((cap, depth, channels)),
                per_step,
                per_step,
                per_step,
                pl.BlockSpec((tile, depth, 2 * steps), lambda i, _: (i, 0, 0)),
                pl.BlockSpec((tile, steps), lambda i, _: (i, 0)),
                whole((depth, channels)),
                whole((1, channels)),
            ],
            out_specs=(
                per_step,
                pl.BlockSpec((tile, depth, channels), lambda i, _: (i, 0, 0)),
            ),
            scratch_shapes=[pltpu.VMEM((steps, tile, channels), jnp.float32)],
        ),
        compiler_params=pltpu.CompilerParams(vmem_limit_bytes=VMEM_LIMIT),
        cost_estimate=pl.CostEstimate(
            flops=8 * steps * base.size,
            bytes_accessed=4 * base.size + 16 * step.size,
            transcendentals=steps * base.size,
        ),
    )(slot, base, extra, step, act, gate, coef, mask, decay, skip)


def per_device(
    input_steps,
    gate_steps,
    conv_state,
    ssm_state,
    new_slot,
    remaining,
    conv_weight,
    conv_bias,
    coef_proj,
    delta_proj,
    delta_bias,
    decay_log,
    skip_gain,
    out_proj,
):
    groups = lax.axis_size("dp")
    my_group = lax.axis_index("dp")
    row_count, taps_kept, channels = conv_state.shape
    state_len = ssm_state.shape[1]
    steps_total = input_steps.shape[0]
    cap = row_count // groups
    total_rows = new_slot.shape[0]

    target = (new_slot // row_count).reshape(groups, row_count)
    position = jnp.arange(row_count, dtype=jnp.int32)
    earlier = position[None, :] < position[:, None]
    rank = jnp.sum(
        ((target[:, :, None] == target[:, None, :]) & earlier[None]).astype(jnp.int32), axis=2
    )
    source = jnp.broadcast_to(jnp.arange(groups, dtype=jnp.int32)[:, None], rank.shape)
    my_target = lax.dynamic_index_in_dim(target, my_group, 0, keepdims=False)
    my_rank = lax.dynamic_index_in_dim(rank, my_group, 0, keepdims=False)
    leave = jnp.where(
        my_rank < cap, my_target * cap + my_rank, row_count + my_rank - cap
    )
    slots = jnp.arange(row_count + cap, dtype=jnp.int32)
    send_index = jnp.sum(
        jnp.where(slots[:, None] == leave[None, :], position[None, :], 0), axis=1
    )
    arrive = jnp.where(rank < cap, source * cap + rank, row_count + rank - cap)
    here = (new_slot[None, :] == (my_group * row_count + position)[:, None])
    slot = jnp.sum(jnp.where(here, arrive.reshape(1, total_rows), 0), axis=1)
    remain_new = jnp.sum(jnp.where(here, remaining[None, :], 0), axis=1)
    group_ids = jnp.arange(groups, dtype=jnp.int32)
    is_extra = (rank == cap).reshape(1, total_rows)
    extra_from = jnp.sum(
        jnp.where(
            is_extra & (target.reshape(1, total_rows) == group_ids[:, None]),
            source.reshape(1, total_rows),
            0,
        ),
        axis=1,
    )

    def exchange(block):
        return lax.all_to_all(block, "dp", split_axis=0, concat_axis=0, tiled=True)

    ssm_base, ssm_extra = pack(send_index, ssm_state, groups)
    conv_packed = conv_state[send_index]
    extra = jnp.concatenate([ssm_extra, conv_packed[row_count:]], axis=1)
    extra = extra.reshape(cap, state_len + taps_kept, groups, channels // groups)
    extra = exchange(extra.transpose(2, 0, 1, 3))
    extra = exchange(extra[extra_from])
    extra = extra.transpose(1, 2, 0, 3).reshape(cap, state_len + taps_kept, channels)
    conv_base = exchange(conv_packed[:row_count])
    ssm_base = exchange(ssm_base)
    ssm_extra = extra[:, :state_len]

    small = jnp.concatenate([coef_proj.T, delta_proj], axis=0)
    small = lax.all_gather(small, "dp", axis=0, tiled=False)
    coef_width = coef_proj.shape[1]
    coef_whole = small[:, :coef_width].reshape(groups * coef_width, channels)
    delta_whole = small[:, coef_width:].reshape(-1, channels)
    rank_len = delta_whole.shape[0]
    out_whole = lax.all_gather(out_proj, "dp", axis=0, tiled=False)

    conv_moved = jnp.concatenate([conv_base, extra[:, state_len:]], axis=0)[slot]
    sequence = [conv_moved[:, k] for k in range(taps_kept)]
    sequence += [input_steps[t] for t in range(steps_total)]
    wide = [entry.astype(jnp.float32) for entry in sequence]
    activated = jnp.stack(
        [
            jax.nn.silu(
                sum(wide[t + k] * conv_weight[k][None] for k in range(taps_kept + 1)) + conv_bias
            )
            for t in range(steps_total)
        ]
    )
    partial_value = lax.dot_general(
        activated.reshape(steps_total * row_count, channels).astype(jnp.bfloat16),
        coef_whole,
        (((1,), (1,)), ((), ())),
        preferred_element_type=jnp.float32,
    )
    low_rank = lax.psum(partial_value.astype(jnp.bfloat16), "mp")
    coef = low_rank[:, rank_len:].astype(jnp.float32)
    coef = coef.reshape(steps_total, row_count, 2, state_len)
    coef = coef.transpose(1, 3, 0, 2).reshape(row_count, state_len, 2 * steps_total)
    active = remain_new[:, None] > jnp.arange(steps_total, dtype=jnp.int32)[None, :]
    step_size = jax.nn.softplus(
        jnp.dot(low_rank[:, :rank_len], delta_whole, preferred_element_type=jnp.float32)
        + delta_bias
    ).reshape(steps_total, row_count, channels)
    step_size = jnp.where(active.T[:, :, None], step_size, 0.0)

    mixed, ssm_final = scan(
        slot,
        ssm_base,
        ssm_extra,
        step_size,
        activated,
        gate_steps,
        coef,
        active.astype(jnp.int32),
        -jnp.exp(decay_log),
        skip_gain[None],
    )
    last = jnp.minimum(remain_new, steps_total)[:, None]
    window = []
    for k in range(taps_kept):
        entry = sequence[k]
        for t in range(1, steps_total + 1):
            entry = jnp.where(last == t, sequence[k + t], entry)
        window.append(entry)
    conv_final = jnp.stack(window, axis=1)

    partial_mix = jnp.einsum(
        "rc,gcd->rgd",
        mixed.reshape(steps_total * row_count, channels),
        out_whole,
        preferred_element_type=jnp.float32,
    ).reshape(steps_total * row_count, -1)
    summed = lax.psum_scatter(
        partial_mix.astype(jnp.bfloat16), "mp", scatter_dimension=1, tiled=True
    )
    layer_out = summed.reshape(steps_total, row_count, summed.shape[1])
    return (layer_out, conv_final, ssm_final)


def solution(mesh):
    return jax.shard_map(
        per_device,
        mesh=mesh,
        in_specs=(
            P(None, "dp", "mp"),
            P(None, "dp", "mp"),
            P("dp", None, "mp"),
            P("dp", None, "mp"),
            P(),
            P(),
            P(None, "mp"),
            P("mp"),
            P("mp", "dp"),
            P("dp", "mp"),
            P("mp"),
            P(None, "mp"),
            P("mp"),
            P("mp", "dp"),
        ),
        out_specs=(P(None, "dp", "mp"), P("dp", None, "mp"), P("dp", None, "mp")),
        check_vma=False,
    )
```

time: 792 us -> 629 us (0.79)
  waiting for transfers between devices: 556 us -> 461 us
  other arithmetic: 97.4 us -> 16.5 us
  Pallas kernels: 0 us -> 38.6 us
  local copies, waits for them, and re-layouts: 77.8 us -> 56.2 us
    all_gather x3 -> x2, waiting for transfers between devices: 436 us -> 85.9 us  [the longest x1 85.9 us: per_device(): out_whole = lax.all_gather(out_proj, 'dp', axis=0, tiled=False)]
    all_to_all x2 -> x4, waiting for transfers between devices: 105 us -> 319 us  [exchange(): return lax.all_to_all(block, 'dp', split_axis=0, concat_axis=0, tiled=True)]
    reduce_sum x3 -> x4, other arithmetic: 54.9 us -> 0.78 us  [the longest x1 0.35 us: per_device(): jnp.sum(((target[:, :, None] == target[:, None, :]) & earlier[None]).asty...]
    pallas_call x0 -> x2, Pallas kernels: none -> 38.6 us  [the longest x1 31.2 us: scan(): pl.pallas_call(scan_kernel, out_shape=(jax.ShapeDtypeStruct((steps, rows,...]
    scatter x3 -> x0, local copies, waits for them, and re-layouts: 33.2 us -> none  [the longest x2 29.8 us: relocate(): jnp.zeros((groups * capacity, depth, channels), state.dtype).at[send_index]]
    convert_element_type x6 -> x2, other arithmetic: 31 us -> 1.63 us  [the longest x1 1.55 us: per_device(): activated.reshape(steps_total * row_count, channels).astype(jnp.bfloat16)]
    reduce_scatter x1, waiting for transfers between devices: 10.7 us -> 33.5 us  [per_device(): lax.psum_scatter(partial_mix.astype(jnp.bfloat16), 'mp', scatter_dimensio...]
    dot_general x0 -> x1, local copies, waits for them, and re-layouts: none -> 21.8 us  [per_device(): jnp.einsum('rc,gcd->rgd', mixed.reshape(steps_total * row_count, channels...]
  transfers between devices with their start and end apart: 7 -> 8, of which waited for: 7 -> 7; matrix products, arithmetic and copies ran while one was open for 17% -> 6% of each run, Pallas kernels for 0% -> 5%
where the time goes in v1:
time: 629 us; the launch traced here: 628 us
  waiting for transfers between devices  461 us (73%)
  local copies, waits for them, and re-layouts  56.2 us (9%)
  Pallas kernels  38.6 us (6%)
  starting transfers between devices  20.9 us (3%)
  matrix products  20 us (3%)
  other arithmetic  16.5 us (3%)
  between operations  14.3 us (2%)
    all_to_all x4, waiting for transfers between devices, exchange(): return lax.all_to_all(block, 'dp', split_axis=0, concat_axis=0, tiled=True)  319 us
    all_gather x1, waiting for transfers between devices, per_device(): out_whole = lax.all_gather(out_proj, 'dp', axis=0, tiled=False)  85.9 us
    reduce_scatter x1, waiting for transfers between devices, per_device(): lax.psum_scatter(partial_mix.astype(jnp.bfloat16), 'mp', scatter_dimensio...  33.5 us
    pallas_call x1, Pallas kernels, scan(): pl.pallas_call(scan_kernel, out_shape=(jax.ShapeDtypeStruct((steps, rows,...  31.2 us
    psum x1, waiting for transfers between devices, per_device(): low_rank = lax.psum(partial_value.astype(jnp.bfloat16), 'mp')  22 us
    dot_general x1, local copies, waits for them, and re-layouts, per_device(): jnp.einsum('rc,gcd->rgd', mixed.reshape(steps_total * row_count, channels...  21.8 us
    all_to_all x4, starting transfers between devices, exchange(): return lax.all_to_all(block, 'dp', split_axis=0, concat_axis=0, tiled=True)  20.3 us
  transfers between devices with their start and end apart: 8, of which 7 were waited for; matrix products, arithmetic and copies ran while one was open for 6% of the time, Pallas kernels for 5%

profile of v1, /device:TPU:0, one launch (start us, length us, event | category | flops | bytes accessed | tf_op | source)
XLA Modules:
  0.0 627.6 jit_solution(11775413165477610921)
XLA Ops:
  8.6 4.9 gather_fusion
  13.7 7.4 %shard_map.157 = (bf16[96,16,2048]{2,1,0:T(8,128)(2,1)}, bf16[12,16,2048]{2,1,0:T(8,128)(2,1)S(1)}) custom-call(s32[108]{0:T(128)S(1)} %select_reduce_fusion.index_ref, bf16[96,16,2048]{2,1,0:T(8,128)(2,1)} %state_ref.1), custom_call_target="tpu_custom_call" | custom-call | bytes 12582912 | tf_op jit(solution)/shard_map/pallas_call | solution.py:27
  25.2 7.3 %all-to-all-start.1 = ((bf16[8,12,19,256]{3,2,1,0:T(8,128)(2,1)}), bf16[8,12,19,256]{3,2,1,0:T(8,128)(2,1)S(1)}, u32[]{:S(2)}, u32[]{:S(2)}) async-start(bf16[8,12,19,256]{3,2,1,0:T(8,128)(2,1)} %bitcast.89), calls=%async_computation.1 | async-start | bytes 2359296 | tf_op jit(solution)/shard_map/all_to_all | solution.py:205
  33.7 42.9 %all-to-all-done.1 = bf16[8,12,19,256]{3,2,1,0:T(8,128)(2,1)S(1)} async-done(((bf16[8,12,19,256]{3,2,1,0:T(8,128)(2,1)}), bf16[8,12,19,256]{3,2,1,0:T(8,128)(2,1)S(1)}, u32[]{:S(2)}, u32[]{:S(2)}) %all-to-all-start.1) | async-done | bytes 933920 | tf_op jit(solution)/shard_map/all_to_all | solution.py:205
  78.3 4.6 all-to-all-start.2
  82.9 2.2 copy.52
  85.1 57.3 %all-to-all-done.2 = bf16[8,12,19,256]{3,2,1,0:T(8,128)(2,1)S(1)} async-done(((bf16[8,12,19,256]{3,2,1,0:T(8,128)(2,1)}), bf16[8,12,19,256]{3,2,1,0:T(8,128)(2,1)S(1)}, u32[]{:S(2)}, u32[]{:S(2)}) %all-to-all-start.2) | async-done | bytes 933920 | tf_op jit(solution)/shard_map/all_to_all | solution.py:205
  142.4 3.6 all-to-all-start.3
  150.9 32.0 %all-to-all-done.3 = bf16[96,3,2048]{2,1,0:T(4,128)(2,1)S(1)} async-done(((bf16[96,3,2048]{2,1,0:T(4,128)(2,1)}), bf16[96,3,2048]{2,1,0:T(4,128)(2,1)S(1)}, u32[]{:S(2)}, u32[]{:S(2)}) %all-to-all-start.3) | async-done | bytes 1179680 | tf_op jit(solution)/shard_map/all_to_all | solution.py:205
  182.9 2.4 pad_maximum_fusion.1
  185.3 3.4 gather_fusion.2
  198.1 2.1 reshape.564
  200.2 4.2 convolution_convert_fusion.1
  205.2 4.9 all-to-all-start
  210.6 3.7 slice.103
  214.3 22.0 %all-reduce.2.cloned.1.call-done = bf16[384,544]{0,1:T(8,128)(2,1)} async-done(((bf16[384,544]{0,1:T(8,128)(2,1)}), bf16[384,544]{0,1:T(8,128)(2,1)}) %all-reduce.2.cloned.1.call-update) | async-done | bytes 417808 | tf_op jit(solution)/shard_map/psum | solution.py:244
  237.7 4.3 compare_select_fusion
  242.0 3.3 pad_maximum_fusion
  245.3 186.9 %all-to-all-done.base_ref = bf16[96,16,2048]{2,1,0:T(8,128)(2,1)} async-done(((bf16[96,16,2048]{2,1,0:T(8,128)(2,1)}), bf16[96,16,2048]{2,1,0:T(8,128)(2,1)}, u32[]{:S(2)}, u32[]{:S(2)}) %all-to-all-start) | async-done | bytes 6291488 | tf_op jit(solution)/shard_map/all_to_all | solution.py:205
  432.3 31.2 %shard_map.158 = (bf16[4,96,2048]{2,1,0:T(8,128)(2,1)S(1)}, bf16[96,16,2048]{2,1,0:T(8,128)(2,1)}) custom-call(s32[96]{0:T(128)S(1)} %get-tuple-element.12.slot_ref, bf16[96,16,2048]{2,1,0:T(8,128)(2,1)} %all-to-all-done.base_ref, bf16[12,16,2048]{2,1,0:T(8,128)(2,1)S(1)} %slice.95.extra_ref, f32[4,96,2048]{2,1,0:T(8,128)} %get-tuple-element.34.step_ref, ...), custom_call_target="tpu_custom_call" | custom-call | flops 100663296 | bytes 25165824 | tf_op jit(solution)/shard_map/pallas_call | solution.py:114
  464.6 85.9 %all-gather.6.cloned.1.call-done = bf16[16384,512]{1,0:T(8,128)(2,1)} async-done(((bf16[2048,512]{1,0:T(8,128)(2,1)}), bf16[16384,512]{1,0:T(8,128)(2,1)}) %all-gather.6.cloned.1.call-update) | async-done | bytes 16777232 | tf_op jit(solution)/shard_map/all_gather | solution.py:224
  550.6 21.8 %copy.58 = bf16[8,512,2048]{2,1,0:T(8,128)(2,1)} copy(bf16[8,512,2048]{1,2,0:T(8,128)(2,1)} %bitcast.86) | data formatting | bytes 33554432 | tf_op jit(solution)/shard_map/rc,gcd->rgd/dot_general | solution.py:276
  572.4 11.5 %convolution_convert_fusion = bf16[384,4096]{1,0:T(8,128)(2,1)} fusion(bf16[384,2048]{1,0:T(8,128)(2,1)S(1)} %bitcast.85, bf16[4096,2048]{1,0:T(8,128)(2,1)} %bitcast.87), kind=kOutput, calls=%fused_computation.4 | convolution fusion | flops 6444023808 | bytes 21495808 | tf_op jit(solution)/shard_map/rc,gcd->rgd/dot_general | solution.py:276
  587.6 33.5 %reduce-scatter.2.cloned.1.call-done = bf16[384,1024]{1,0:T(8,128)(2,1)} async-done(((bf16[384,4096]{1,0:T(8,128)(2,1)}), bf16[384,1024]{1,0:T(8,128)(2,1)}) %reduce-scatter.2.cloned.1.call-update) | async-done | bytes 786448 | tf_op jit(solution)/shard_map/reduce_scatter | solution.py:282
  (122 shorter events, 30.3 us)
Async XLA Ops:
  23.9 8.6 %copy-start.23 = (bf16[2048,68]{0,1:T(8,128)(2,1)S(1)}, bf16[2048,68]{0,1:T(8,128)(2,1)}, u32[]{:S(2)}) copy-start(bf16[2048,68]{0,1:T(8,128)(2,1)} %param.22) | copy-start | bytes 835588
  23.9 8.6 %copy-start.24 = (bf16[64,2048]{1,0:T(8,128)(2,1)S(1)}, bf16[64,2048]{1,0:T(8,128)(2,1)}, u32[]{:S(2)}) copy-start(bf16[64,2048]{1,0:T(8,128)(2,1)} %param.23) | copy-start | bytes 786436
  25.2 51.5 %all-to-all-start.1 = ((bf16[8,12,19,256]{3,2,1,0:T(8,128)(2,1)}), bf16[8,12,19,256]{3,2,1,0:T(8,128)(2,1)S(1)}, u32[]{:S(2)}, u32[]{:S(2)}) async-start(bf16[8,12,19,256]{3,2,1,0:T(8,128)(2,1)} %bitcast.89), calls=%async_computation.1 | async-start | bytes 2359296 | tf_op jit(solution)/shard_map/all_to_all | solution.py:205
  32.4 164.1 %all-gather.8.cloned.1.call-start = ((), (), s32[]{:S(2)}) async-start(), calls=%async_computation.8 | async-start | bytes 5013504 | tf_op jit(solution)/shard_map/all_gather | solution.py:219
  78.3 64.1 %all-to-all-start.2 = ((bf16[8,12,19,256]{3,2,1,0:T(8,128)(2,1)}), bf16[8,12,19,256]{3,2,1,0:T(8,128)(2,1)S(1)}, u32[]{:S(2)}, u32[]{:S(2)}) async-start(bf16[8,12,19,256]{3,2,1,0:T(8,128)(2,1)} %gather_fusion.1), calls=%async_computation.2 | async-start | bytes 2359296 | tf_op jit(solution)/shard_map/all_to_all | solution.py:205
  85.1 61.3 %copy-start.27 = (s32[768]{0:T(1024)S(1)}, s32[768]{0:T(1024)}, u32[]{:S(2)}) copy-start(s32[768]{0:T(1024)} %param.18) | copy-start | bytes 9220
  85.1 61.3 %copy-start.29 = (s32[768]{0:T(1024)S(1)}, s32[768]{0:T(1024)}, u32[]{:S(2)}) copy-start(s32[768]{0:T(1024)} %param.19) | copy-start | bytes 9220
  85.1 61.5 %copy-start.26 = (f32[4,2048]{1,0:T(4,128)S(1)}, f32[4,2048]{1,0:T(4,128)}, u32[]{:S(2)}) copy-start(f32[4,2048]{1,0:T(4,128)} %param.20) | copy-start | bytes 98308
  142.4 40.5 %all-to-all-start.3 = ((bf16[96,3,2048]{2,1,0:T(4,128)(2,1)}), bf16[96,3,2048]{2,1,0:T(4,128)(2,1)S(1)}, u32[]{:S(2)}, u32[]{:S(2)}) async-start(bf16[96,3,2048]{2,1,0:T(4,128)(2,1)} %copy.52), calls=%async_computation.3 | async-start | bytes 3145728 | tf_op jit(solution)/shard_map/all_to_all | solution.py:205
  146.0 90.4 %all-reduce.2.cloned.1.call-start = ((), (), s32[]{:S(2)}) async-start(), calls=%async_computation.5 | async-start | bytes 835584 | tf_op jit(solution)/shard_map/psum | solution.py:244
  204.4 346.1 %all-gather.6.cloned.1.call-start = ((), (), s32[]{:S(2)}) async-start(), calls=%async_computation.7 | async-start | bytes 18874368 | tf_op jit(solution)/shard_map/all_gather | solution.py:224
  205.2 5.3 copy-start.25
  205.2 5.3 copy-start.17
  205.2 227.0 %all-to-all-start = ((bf16[96,16,2048]{2,1,0:T(8,128)(2,1)}), bf16[96,16,2048]{2,1,0:T(8,128)(2,1)}, u32[]{:S(2)}, u32[]{:S(2)}) async-start(bf16[96,16,2048]{2,1,0:T(8,128)(2,1)} %get-tuple-element.7), calls=%async_computation | async-start | bytes 12582912 | tf_op jit(solution)/shard_map/all_to_all | solution.py:205
  210.1 410.9 %reduce-scatter.2.cloned.1.call-start = ((), (), s32[]{:S(2)}) async-start(), calls=%async_computation.6 | async-start | bytes 3932160 | tf_op jit(solution)/shard_map/reduce_scatter | solution.py:282
  210.6 27.0 %copy-start.30 = (f32[2048]{0:T(1024)S(1)}, f32[2048]{0:T(1024)}, u32[]{:S(2)}) copy-start(f32[2048]{0:T(1024)} %param.24) | copy-start | bytes 24580
  237.6 4.3 copy-start.9
  237.6 4.3 copy-start.11
  237.6 4.3 copy-start.13
  237.7 4.3 copy-start.15
  242.0 190.2 %copy-start.2 = (bf16[4,96,2048]{2,1,0:T(8,128)(2,1)S(1)}, bf16[4,96,2048]{2,1,0:T(8,128)(2,1)}, u32[]{:S(2)}) copy-start(bf16[4,96,2048]{2,1,0:T(8,128)(2,1)} %gate_ref.1) | copy-start | bytes 4718596
  242.0 190.2 %copy-start.3 = (f32[2048]{0:T(1024)S(1)}, f32[2048]{0:T(1024)}, u32[]{:S(2)}) copy-start(f32[2048]{0:T(1024)} %param.26) | copy-start | bytes 24580
  550.6 21.8 %copy-start.5 = (bf16[4,96,2048]{2,1,0:T(8,128)(2,1)S(1)}, bf16[4,96,2048]{2,1,0:T(8,128)(2,1)}, u32[]{:S(2)}) copy-start(bf16[4,96,2048]{2,1,0:T(8,128)(2,1)} %copy-done.4) | copy-start | bytes 4718596
  585.5 35.6 %copy-start.1 = (bf16[96,3,2048]{2,0,1:T(8,128)(2,1)S(1)}, bf16[96,3,2048]{2,0,1:T(8,128)(2,1)}, u32[]{:S(2)}) copy-start(bf16[96,3,2048]{2,0,1:T(8,128)(2,1)} %param.16) | copy-start | bytes 3538948
  (16 other events, 26.5 us)
Sparse Core Ops, SparseCore 0:
  35.4 112.4 all-gather.7
  204.6 31.7 all-reduce.1
  238.7 311.8 all-gather.5
  584.0 36.9 reduce-scatter.1

commit v2 on v1

--- a/solution.py
+++ b/solution.py
@@ -1,3 +1,5 @@
+import functools
+
 import jax
 import jax.numpy as jnp
 from jax import lax
@@ -146,6 +148,214 @@
     )(slot, base, extra, step, act, gate, coef, mask, decay, skip)
 
 
+def remote(src, dst, send_sem, recv_sem, peer):
+    return pltpu.make_async_remote_copy(
+        src_ref=src,
+        dst_ref=dst,
+        send_sem=send_sem,
+        recv_sem=recv_sem,
+        device_id={"dp": peer},
+        device_id_type=pl.DeviceIdType.MESH,
+    )
+
+
+def move_kernel(
+    groups,
+    inner,
+    from_ref,
+    piece_ref,
+    conv_ref,
+    small_ref,
+    ssm_ref,
+    out_ref,
+    piece_out,
+    conv_out,
+    small_all,
+    ssm_out,
+    out_all,
+    held,
+    passed,
+    own_sem,
+    send_sem,
+    recv_sem,
+    gather_send,
+    gather_recv,
+):
+    me = lax.axis_index("dp")
+    outer = groups // inner
+    mine_z = me // inner
+    mine_x = me % inner
+    barrier = pltpu.get_barrier_semaphore()
+    for k in range(1, groups):
+        pl.semaphore_signal(
+            barrier,
+            inc=1,
+            device_id={"dp": (me + k) % groups},
+            device_id_type=pl.DeviceIdType.MESH,
+        )
+    pl.semaphore_wait(barrier, groups - 1)
+
+    def exchange(kind, src, dst):
+        copies = []
+        for k in range(1, groups):
+            peer = (me + k) % groups
+            copy = remote(
+                src.at[peer], dst.at[me], send_sem.at[kind, k], recv_sem.at[kind, k], peer
+            )
+            copy.start()
+            copies.append(copy)
+        own = pltpu.make_async_copy(src.at[me], dst.at[me], own_sem.at[kind])
+        own.start()
+        return copies, own
+
+    def finish(started):
+        copies, own = started
+        for copy in copies:
+            copy.wait_recv()
+        own.wait()
+
+    def gather_copy(kind, src, dst, origin, lane, peer):
+        return remote(
+            src, dst.at[origin], gather_send.at[kind, origin, lane], gather_recv.at[kind, origin], peer
+        )
+
+    def across(kind, src, dst, origin):
+        for k in range(1, inner):
+            peer = mine_z * inner + (mine_x + k) % inner
+            gather_copy(kind, src, dst, origin, 1 + k, peer).start()
+
+    def along(kind, src, dst, origin, up):
+        peer = me + inner if up else me - inner
+        room = mine_z + 1 < outer if up else mine_z >= 1
+
+        @pl.when(room)
+        def _():
+            gather_copy(kind, src, dst, origin, 0 if up else 1, peer).start()
+
+    def gather_first(kind, src, dst):
+        along(kind, src, dst, me, True)
+        along(kind, src, dst, me, False)
+        across(kind, src, dst, me)
+        own = pltpu.make_async_copy(src, dst.at[me], own_sem.at[kind])
+        own.start()
+        return own
+
+    def arrived(kind, dst, origin):
+        gather_copy(kind, dst.at[origin], dst, origin, 0, me).wait_recv()
+
+    def gather_rest(kind, dst):
+        for s in range(1, outer):
+            for up in (True, False):
+                origin = me - s * inner if up else me + s * inner
+                there = mine_z >= s if up else mine_z + s < outer
+
+                @pl.when(there)
+                def _():
+                    arrived(kind, dst, origin)
+                    along(kind, dst.at[origin], dst, origin, up)
+                    across(kind, dst.at[origin], dst, origin)
+
+    def gather_end(kind, src, dst, own):
+        for z in range(outer):
+            for k in range(1, inner):
+                arrived(kind, dst, z * inner + (mine_x + k) % inner)
+        own.wait()
+        for z in range(outer):
+            origin = z * inner + mine_x
+
+            @pl.when((mine_z >= z) & (mine_z + 1 < outer))
+            def _():
+                gather_copy(kind, src, dst, origin, 0, me).wait_send()
+
+            @pl.when((mine_z <= z) & (mine_z >= 1))
+            def _():
+                gather_copy(kind, src, dst, origin, 1, me).wait_send()
+
+            for k in range(1, inner):
+                gather_copy(kind, src, dst, origin, 1 + k, me).wait_send()
+
+    first = exchange(0, piece_ref, held)
+    conv = exchange(1, conv_ref, conv_out)
+    small_own = gather_first(4, small_ref, small_all)
+    ssm = exchange(2, ssm_ref, ssm_out)
+    out_own = gather_first(5, out_ref, out_all)
+    finish(first)
+    for h in range(groups):
+        passed[h] = held[from_ref[h]]
+    second = exchange(3, passed, piece_out)
+    gather_rest(4, small_all)
+    gather_rest(5, out_all)
+    gather_end(4, small_ref, small_all, small_own)
+    finish(conv)
+    finish(second)
+    gather_end(5, out_ref, out_all, out_own)
+    finish(ssm)
+    for copies, _ in (first, conv, ssm, second):
+        for copy in copies:
+            copy.wait_send()
+
+
+def move(extra_from, pieces, conv, small, ssm, out):
+    groups = pieces.shape[0]
+    inner = 1
+    while inner * inner * 4 <= groups:
+        inner *= 2
+    held = pl.BlockSpec(memory_space=pl.ANY)
+
+    def like(array):
+        return jax.ShapeDtypeStruct(array.shape, array.dtype)
+
+    def gathered(array):
+        return jax.ShapeDtypeStruct((groups,) + array.shape, array.dtype)
+
+    return pl.pallas_call(
+        functools.partial(move_kernel, groups, inner),
+        out_shape=(like(pieces), like(conv), gathered(small), like(ssm), gathered(out)),
+        in_specs=[pl.BlockSpec(memory_space=pltpu.SMEM)] + [held] * 5,
+        out_specs=(held,) * 5,
+        scratch_shapes=[
+            pltpu.VMEM(pieces.shape, pieces.dtype),
+            pltpu.VMEM(pieces.shape, pieces.dtype),
+            pltpu.SemaphoreType.DMA((6,)),
+            pltpu.SemaphoreType.DMA((4, groups)),
+            pltpu.SemaphoreType.DMA((4, groups)),
+            pltpu.SemaphoreType.DMA((6, groups, 1 + inner)),
+            pltpu.SemaphoreType.DMA((6, groups)),
+        ],
+        compiler_params=pltpu.CompilerParams(collective_id=0, has_side_effects=True),
+        cost_estimate=pl.CostEstimate(
+            flops=0, bytes_accessed=4 * groups * out.size, transcendentals=0
+        ),
+    )(extra_from, pieces, conv, small, ssm, out)
+
+
+def mix_kernel(rows_ref, weight_ref, out_ref):
+    out_ref[...] = jnp.dot(
+        rows_ref[...], weight_ref[0], preferred_element_type=jnp.float32
+    ).astype(out_ref.dtype)
+
+
+def mix(rows, weights):
+    groups, channels, width = weights.shape
+    count = rows.shape[0]
+    return pl.pallas_call(
+        mix_kernel,
+        out_shape=jax.ShapeDtypeStruct((count, groups * width), jnp.bfloat16),
+        grid=(groups,),
+        in_specs=[
+            pl.BlockSpec((count, channels), lambda g: (0, 0)),
+            pl.BlockSpec((1, channels, width), lambda g: (g, 0, 0)),
+        ],
+        out_specs=pl.BlockSpec((count, width), lambda g: (0, g)),
+        compiler_params=pltpu.CompilerParams(vmem_limit_bytes=VMEM_LIMIT),
+        cost_estimate=pl.CostEstimate(
+            flops=2 * count * weights.size,
+            bytes_accessed=2 * weights.size,
+            transcendentals=0,
+        ),
+    )(rows, weights)
+
+
 def per_device(
     input_steps,
     gate_steps,
@@ -201,29 +411,46 @@
         axis=1,
     )
 
-    def exchange(block):
-        return lax.all_to_all(block, "dp", split_axis=0, concat_axis=0, tiled=True)
+    def padded(rows, count):
+        return jnp.pad(rows, ((0, 0),) * (rows.ndim - 2) + ((0, count - rows.shape[-2]), (0, 0)))
 
     ssm_base, ssm_extra = pack(send_index, ssm_state, groups)
     conv_packed = conv_state[send_index]
-    extra = jnp.concatenate([ssm_extra, conv_packed[row_count:]], axis=1)
-    extra = extra.reshape(cap, state_len + taps_kept, groups, channels // groups)
-    extra = exchange(extra.transpose(2, 0, 1, 3))
-    extra = exchange(extra[extra_from])
-    extra = extra.transpose(1, 2, 0, 3).reshape(cap, state_len + taps_kept, channels)
-    conv_base = exchange(conv_packed[:row_count])
-    ssm_base = exchange(ssm_base)
-    ssm_extra = extra[:, :state_len]
-
-    small = jnp.concatenate([coef_proj.T, delta_proj], axis=0)
-    small = lax.all_gather(small, "dp", axis=0, tiled=False)
+    ssm_rows, conv_rows = cap * state_len, cap * taps_kept
+    depth = -(-(ssm_rows + conv_rows) // (16 * groups)) * 16
+    extra = jnp.concatenate(
+        [
+            ssm_extra.reshape(ssm_rows, channels),
+            conv_packed[row_count:].reshape(conv_rows, channels),
+        ],
+        axis=0,
+    )
+    pieces = padded(extra, groups * depth).reshape(groups, depth, channels)
+    conv_depth = -(-conv_rows // 16) * 16
+    conv_blocks = padded(
+        conv_packed[:row_count].reshape(groups, conv_rows, channels), conv_depth
+    )
     coef_width = coef_proj.shape[1]
+    coef_depth = -(-coef_width // 16) * 16
+    small = jnp.concatenate([padded(coef_proj.T, coef_depth), delta_proj], axis=0)
+    extra, conv_base, small, ssm_base, out_whole = move(
+        extra_from,
+        pieces,
+        conv_blocks,
+        small,
+        ssm_base.reshape(groups, ssm_rows, channels),
+        out_proj,
+    )
+    extra = extra.reshape(groups * depth, channels)
+    ssm_base = ssm_base.reshape(row_count, state_len, channels)
+    ssm_extra = extra[:ssm_rows].reshape(cap, state_len, channels)
+    conv_extra = extra[ssm_rows : ssm_rows + conv_rows].reshape(cap, taps_kept, channels)
+    conv_base = conv_base[:, :conv_rows].reshape(row_count, taps_kept, channels)
     coef_whole = small[:, :coef_width].reshape(groups * coef_width, channels)
-    delta_whole = small[:, coef_width:].reshape(-1, channels)
+    delta_whole = small[:, coef_depth:].reshape(-1, channels)
     rank_len = delta_whole.shape[0]
-    out_whole = lax.all_gather(out_proj, "dp", axis=0, tiled=False)
-
-    conv_moved = jnp.concatenate([conv_base, extra[:, state_len:]], axis=0)[slot]
+
+    conv_moved = jnp.concatenate([conv_base, conv_extra], axis=0)[slot]
     sequence = [conv_moved[:, k] for k in range(taps_kept)]
     sequence += [input_steps[t] for t in range(steps_total)]
     wide = [entry.astype(jnp.float32) for entry in sequence]
@@ -273,14 +500,9 @@
         window.append(entry)
     conv_final = jnp.stack(window, axis=1)
 
-    partial_mix = jnp.einsum(
-        "rc,gcd->rgd",
-        mixed.reshape(steps_total * row_count, channels),
-        out_whole,
-        preferred_element_type=jnp.float32,
-    ).reshape(steps_total * row_count, -1)
+    partial_mix = mix(mixed.reshape(steps_total * row_count, channels), out_whole)
     summed = lax.psum_scatter(
-        partial_mix.astype(jnp.bfloat16), "mp", scatter_dimension=1, tiled=True
+        partial_mix, "mp", scatter_dimension=1, tiled=True
     )
     layer_out = summed.reshape(steps_total, row_count, summed.shape[1])
     return (layer_out, conv_final, ssm_final)

time: 629 us -> 650 us (1.033)
  Pallas kernels: 38.6 us -> 509 us
  waiting for transfers between devices: 461 us -> 61.3 us
  starting transfers between devices: 20.9 us -> 0.3 us
  local copies, waits for them, and re-layouts: 56.2 us -> 41.2 us
  matrix products: 20 us -> 6.42 us
    pallas_call x0 -> x2, Pallas kernels: none -> 470 us  [the longest x1 457 us: move(): pl.pallas_call(functools.partial(move_kernel, groups, inner), out_shape=(...]
    all_to_all x4 -> x0, waiting for transfers between devices: 319 us -> none  [exchange(): return lax.all_to_all(block, 'dp', split_axis=0, concat_axis=0, tiled=True)]
    all_gather x2 -> x0, waiting for transfers between devices: 85.9 us -> none  [the longest x1 85.9 us: per_device(): out_whole = lax.all_gather(out_proj, 'dp', axis=0, tiled=False)]
    dot_general x1 -> x0, local copies, waits for them, and re-layouts: 21.8 us -> none  [per_device(): jnp.einsum('rc,gcd->rgd', mixed.reshape(steps_total * row_count, channels...]
    all_to_all x4 -> x0, starting transfers between devices: 20.3 us -> none  [exchange(): return lax.all_to_all(block, 'dp', split_axis=0, concat_axis=0, tiled=True)]
    dot_general x1 -> x0, matrix products: 11.5 us -> none  [per_device(): jnp.einsum('rc,gcd->rgd', mixed.reshape(steps_total * row_count, channels...]
  transfers between devices with their start and end apart: 8 -> 2, of which waited for: 7 -> 2; matrix products, arithmetic and copies ran while one was open for 6% -> 1% of each run, Pallas kernels for 5% -> 0%
where the time goes in v2:
time: 650 us
  Pallas kernels  509 us (78%)
  waiting for transfers between devices  61.3 us (9%)
  local copies, waits for them, and re-layouts  41.2 us (6%)
  other arithmetic  17 us (3%)
  between operations  14.5 us (2%)
    pallas_call x1, Pallas kernels, move(): pl.pallas_call(functools.partial(move_kernel, groups, inner), out_shape=(...  457 us
    reduce_scatter x1, waiting for transfers between devices, per_device(): lax.psum_scatter(partial_mix, 'mp', scatter_dimension=1, tiled=True)  34.9 us
    pallas_call x1, Pallas kernels, scan(): pl.pallas_call(scan_kernel, out_shape=(jax.ShapeDtypeStruct((steps, rows,...  31.1 us
    psum x1, waiting for transfers between devices, per_device(): low_rank = lax.psum(partial_value.astype(jnp.bfloat16), 'mp')  26.4 us
  transfers between devices with their start and end apart: 2, of which 2 were waited for; matrix products, arithmetic and copies ran while one was open for 1% of the time, Pallas kernels for 0%

profile of v2, /device:TPU:0, one launch (start us, length us, event | category | flops | bytes accessed | tf_op | source)
XLA Modules:
  0.0 649.6 jit_solution(7673748696849648834)
XLA Ops:
  8.6 4.9 gather_fusion
  15.6 2.3 copy.27
  17.9 2.4 reshape.576
  20.3 7.4 %shard_map.157 = (bf16[96,16,2048]{2,1,0:T(8,128)(2,1)}, bf16[12,16,2048]{2,1,0:T(8,128)(2,1)S(1)}) custom-call(s32[108]{0:T(128)S(1)} %select_reduce_fusion.index_ref, bf16[96,16,2048]{2,1,0:T(8,128)(2,1)} %state_ref.1), custom_call_target="tpu_custom_call" | custom-call | bytes 12582912 | tf_op jit(solution)/shard_map/pallas_call | solution.py:29
  29.2 1.4 pad.13.conv_ref
  31.7 457.4 %shard_map.158 = (bf16[8,32,2048]{2,1,0:T(8,128)(2,1)}, bf16[8,48,2048]{2,1,0:T(8,128)(2,1)}, bf16[8,144,2048]{2,1,0:T(8,128)(2,1)}, bf16[8,192,2048]{2,1,0:T(8,128)(2,1)}, bf16[8,2048,512]{2,1,0:T(8,128)(2,1)}) custom-call(s32[8]{0:T(128)} %select_reduce_fusion.1.from_ref, bf16[8,32,2048]{2,1,0:T(8,128)(2,1)} %bitcast.77, ...), custom_call_target="tpu_custom_call" | custom-call | bytes 33554432 | tf_op jit(solution)/shard_map/pallas_call | solution.py:311
  490.1 2.5 slice.76
  492.7 2.6 reshape.580
  495.2 2.3 pad_maximum_fusion.1
  497.6 3.4 gather_fusion.1
  500.9 2.4 fusion.34
  503.4 3.4 slice.89
  506.8 4.2 reshape.583
  510.9 2.7 fusion.22
  513.6 1.6 divide_multiply_fusion.3
  518.0 2.1 convolution_convert_fusion
  520.5 1.2 slice.75
  521.7 3.2 slice.91
  525.0 26.4 %all-reduce.5.cloned.1.call-done = bf16[384,544]{0,1:T(8,128)(2,1)} async-done(((bf16[384,544]{0,1:T(8,128)(2,1)}), bf16[384,544]{0,1:T(8,128)(2,1)}) %all-reduce.5.cloned.1.call-update) | async-done | bytes 417808 | tf_op jit(solution)/shard_map/psum | solution.py:471
  552.7 4.3 compare_select_fusion
  557.1 3.5 pad_maximum_fusion
  560.6 31.1 %shard_map.159 = (bf16[4,96,2048]{2,1,0:T(8,128)(2,1)S(1)}, bf16[96,16,2048]{2,1,0:T(8,128)(2,1)}) custom-call(s32[96]{0:T(128)S(1)} %get-tuple-element.22.slot_ref, bf16[96,16,2048]{2,1,0:T(8,128)(2,1)} %bitcast.88, bf16[12,16,2048]{2,1,0:T(8,128)(2,1)S(1)} %bitcast.72, f32[4,96,2048]{2,1,0:T(8,128)} %get-tuple-element.44.step_ref, ...), custom_call_target="tpu_custom_call" | custom-call | flops 100663296 | bytes 25165824 | tf_op jit(solution)/shard_map/pallas_call | solution.py:116
  591.6 12.9 %shard_map.160 = bf16[384,4096]{1,0:T(8,128)(2,1)} custom-call(bf16[384,2048]{1,0:T(8,128)(2,1)S(1)} %bitcast.75, bf16[8,2048,512]{2,1,0:T(8,128)(2,1)} %get-tuple-element.19.weight_ref), custom_call_target="tpu_custom_call" | custom-call | flops 6442450944 | bytes 16777216 | tf_op jit(solution)/shard_map/pallas_call | solution.py:341
  607.8 34.9 %reduce-scatter.2.cloned.1.call-done = bf16[384,1024]{1,0:T(8,128)(2,1)} async-done(((bf16[384,4096]{1,0:T(8,128)(2,1)}), bf16[384,1024]{1,0:T(8,128)(2,1)}) %reduce-scatter.2.cloned.1.call-update) | async-done | bytes 786448 | tf_op jit(solution)/shard_map/reduce_scatter | solution.py:504
  (100 shorter events, 14.7 us)
Async XLA Ops:
  7.2 1.5 copy-start
  7.2 544.2 %all-reduce.5.cloned.1.call-start = ((), (), s32[]{:S(2)}) async-start(), calls=%async_computation.1 | async-start | bytes 835584 | tf_op jit(solution)/shard_map/psum | solution.py:471
  13.6 1.5 copy-start.24
  13.6 1.5 copy-start.26
  13.6 1.7 copy-start.23
  20.3 8.0 %copy-start.20 = (bf16[2048,68]{0,1:T(8,128)(2,1)S(1)}, bf16[2048,68]{0,1:T(8,128)(2,1)}, u32[]{:S(2)}) copy-start(bf16[2048,68]{0,1:T(8,128)(2,1)} %param.22) | copy-start | bytes 835588
  20.3 8.0 %copy-start.21 = (bf16[64,2048]{1,0:T(8,128)(2,1)S(1)}, bf16[64,2048]{1,0:T(8,128)(2,1)}, u32[]{:S(2)}) copy-start(bf16[64,2048]{1,0:T(8,128)(2,1)} %param.23) | copy-start | bytes 786436
  20.3 8.9 %copy-start.13 = (bf16[8,36,2048]{2,1,0:T(8,128)(2,1)S(1)}, bf16[8,36,2048]{2,1,0:T(8,128)(2,1)}, u32[]{:S(2)}) copy-start(bf16[8,36,2048]{2,1,0:T(8,128)(2,1)} %reshape.576) | copy-start | bytes 3538948
  506.8 4.2 copy-start.4
  510.9 2.7 copy-start.25
  513.6 1.6 copy-start.14
  513.6 1.6 copy-start.16
  515.3 1.6 copy-start.11
  515.3 2.7 copy-start.18
  520.2 122.6 %reduce-scatter.2.cloned.1.call-start = ((), (), s32[]{:S(2)}) async-start(), calls=%async_computation.2 | async-start | bytes 3932160 | tf_op jit(solution)/shard_map/reduce_scatter | solution.py:504
  521.7 3.2 copy-start.22
  521.7 30.9 %copy-start.27 = (f32[2048]{0:T(1024)S(1)}, f32[2048]{0:T(1024)}, u32[]{:S(2)}) copy-start(f32[2048]{0:T(1024)} %param.24) | copy-start | bytes 24580
  552.7 4.4 copy-start.6
  552.7 4.4 copy-start.8
  552.7 4.4 copy-start.10
  552.7 4.4 copy-start.12
  557.1 3.5 copy-start.2
  557.1 3.5 copy-start.3
  605.7 37.1 %copy-start.1 = (bf16[96,3,2048]{2,0,1:T(8,128)(2,1)S(1)}, bf16[96,3,2048]{2,0,1:T(8,128)(2,1)}, u32[]{:S(2)}) copy-start(bf16[96,3,2048]{2,0,1:T(8,128)(2,1)} %param.16) | copy-start | bytes 3538948
  (6 other events, 6.5 us)
Sparse Core Ops, SparseCore 0:
  520.3 31.0 all-reduce.4
  604.7 37.9 reduce-scatter.1

commit v3 on v2

--- a/solution.py
+++ b/solution.py
@@ -8,6 +8,7 @@
 from jax.sharding import PartitionSpec as P
 
 VMEM_LIMIT = 48 * 1024 * 1024
+CHUNKS = 4
 
 
 def pack_kernel(index_ref, state_ref, base_ref, extra_ref):
@@ -51,6 +52,7 @@
 
 
 def scan_kernel(
+    start,
     slot_ref,
     base_ref,
     extra_ref,
@@ -65,7 +67,7 @@
     final_ref,
     read_ref,
 ):
-    first = pl.program_id(0) * step_ref.shape[1]
+    first = (start + pl.program_id(0)) * step_ref.shape[1]
     rows_total = base_ref.shape[0]
     steps, rows, channels = step_ref.shape
     width = min(512, channels)
@@ -103,47 +105,49 @@
         mix_ref[t] = jnp.where(mask_ref[:, t : t + 1] > 0, mixer, 0.0).astype(mix_ref.dtype)
 
 
-def scan(slot, base, extra, step, act, gate, coef, mask, decay, skip):
+def scan(part, parts, slot, base, extra, step, act, gate, coef, mask, decay, skip):
     rows, depth, channels = base.shape
     steps = step.shape[0]
     tile = 16
+    count = rows // parts
+    start = part * count // tile
     cap = extra.shape[0]
 
     def whole(shape):
         return pl.BlockSpec(shape, lambda i, _: (0,) * len(shape))
 
-    per_step = pl.BlockSpec((steps, tile, channels), lambda i, _: (0, i, 0))
+    per_step = pl.BlockSpec((steps, tile, channels), lambda i, _: (0, start + i, 0))
     return pl.pallas_call(
-        scan_kernel,
+        functools.partial(scan_kernel, start),
         out_shape=(
-            jax.ShapeDtypeStruct((steps, rows, channels), jnp.bfloat16),
-            jax.ShapeDtypeStruct((rows, depth, channels), jnp.bfloat16),
+            jax.ShapeDtypeStruct((steps, count, channels), jnp.bfloat16),
+            jax.ShapeDtypeStruct((count, depth, channels), jnp.bfloat16),
         ),
         grid_spec=pltpu.PrefetchScalarGridSpec(
             num_scalar_prefetch=1,
-            grid=(rows // tile,),
+            grid=(count // tile,),
             in_specs=[
                 whole((rows, depth, channels)),
                 whole((cap, depth, channels)),
                 per_step,
                 per_step,
                 per_step,
-                pl.BlockSpec((tile, depth, 2 * steps), lambda i, _: (i, 0, 0)),
-                pl.BlockSpec((tile, steps), lambda i, _: (i, 0)),
+                pl.BlockSpec((tile, depth, 2 * steps), lambda i, _: (start + i, 0, 0)),
+                pl.BlockSpec((tile, steps), lambda i, _: (start + i, 0)),
                 whole((depth, channels)),
                 whole((1, channels)),
             ],
             out_specs=(
-                per_step,
+                pl.BlockSpec((steps, tile, channels), lambda i, _: (0, i, 0)),
                 pl.BlockSpec((tile, depth, channels), lambda i, _: (i, 0, 0)),
             ),
             scratch_shapes=[pltpu.VMEM((steps, tile, channels), jnp.float32)],
         ),
         compiler_params=pltpu.CompilerParams(vmem_limit_bytes=VMEM_LIMIT),
         cost_estimate=pl.CostEstimate(
-            flops=8 * steps * base.size,
+            flops=8 * steps * base.size // parts,
             bytes_accessed=4 * base.size + 16 * step.size,
-            transcendentals=steps * base.size,
+            transcendentals=steps * base.size // parts,
         ),
     )(slot, base, extra, step, act, gate, coef, mask, decay, skip)
 
@@ -166,12 +170,10 @@
     piece_ref,
     conv_ref,
     small_ref,
-    ssm_ref,
     out_ref,
     piece_out,
     conv_out,
     small_all,
-    ssm_out,
     out_all,
     held,
     passed,
@@ -204,7 +206,7 @@
             )
             copy.start()
             copies.append(copy)
-        own = pltpu.make_async_copy(src.at[me], dst.at[me], own_sem.at[kind])
+        own = pltpu.make_async_copy(src.at[me], dst.at[me], own_sem.at[CHUNKS + 1 + kind])
         own.start()
         return copies, own
 
@@ -243,17 +245,16 @@
     def arrived(kind, dst, origin):
         gather_copy(kind, dst.at[origin], dst, origin, 0, me).wait_recv()
 
-    def gather_rest(kind, dst):
-        for s in range(1, outer):
-            for up in (True, False):
-                origin = me - s * inner if up else me + s * inner
-                there = mine_z >= s if up else mine_z + s < outer
-
-                @pl.when(there)
-                def _():
-                    arrived(kind, dst, origin)
-                    along(kind, dst.at[origin], dst, origin, up)
-                    across(kind, dst.at[origin], dst, origin)
+    def gather_rest(kind, dst, s):
+        for up in (True, False):
+            origin = me - s * inner if up else me + s * inner
+            there = mine_z >= s if up else mine_z + s < outer
+
+            @pl.when(there)
+            def _():
+                arrived(kind, dst, origin)
+                along(kind, dst.at[origin], dst, origin, up)
+                across(kind, dst.at[origin], dst, origin)
 
     def gather_end(kind, src, dst, own):
         for z in range(outer):
@@ -276,26 +277,32 @@
 
     first = exchange(0, piece_ref, held)
     conv = exchange(1, conv_ref, conv_out)
-    small_own = gather_first(4, small_ref, small_all)
-    ssm = exchange(2, ssm_ref, ssm_out)
-    out_own = gather_first(5, out_ref, out_all)
+    small_own = gather_first(CHUNKS, small_ref, small_all)
+    depth = out_ref.shape[0] // CHUNKS
+    parts = [
+        (c, out_ref.at[pl.ds(c * depth, depth)], out_all.at[:, pl.ds(c * depth, depth)])
+        for c in range(CHUNKS)
+    ]
+    out_own = [gather_first(*part) for part in parts]
     finish(first)
     for h in range(groups):
         passed[h] = held[from_ref[h]]
-    second = exchange(3, passed, piece_out)
-    gather_rest(4, small_all)
-    gather_rest(5, out_all)
-    gather_end(4, small_ref, small_all, small_own)
+    second = exchange(2, passed, piece_out)
+    for s in range(1, outer):
+        gather_rest(CHUNKS, small_all, s)
+        for c, _, whole in parts:
+            gather_rest(c, whole, s)
+    gather_end(CHUNKS, small_ref, small_all, small_own)
     finish(conv)
     finish(second)
-    gather_end(5, out_ref, out_all, out_own)
-    finish(ssm)
-    for copies, _ in (first, conv, ssm, second):
+    for (c, part, whole), own in zip(parts, out_own):
+        gather_end(c, part, whole, own)
+    for copies, _ in (first, conv, second):
         for copy in copies:
             copy.wait_send()
 
 
-def move(extra_from, pieces, conv, small, ssm, out):
+def move(extra_from, pieces, conv, small, out):
     groups = pieces.shape[0]
     inner = 1
     while inner * inner * 4 <= groups:
@@ -310,23 +317,23 @@
 
     return pl.pallas_call(
         functools.partial(move_kernel, groups, inner),
-        out_shape=(like(pieces), like(conv), gathered(small), like(ssm), gathered(out)),
-        in_specs=[pl.BlockSpec(memory_space=pltpu.SMEM)] + [held] * 5,
-        out_specs=(held,) * 5,
+        out_shape=(like(pieces), like(conv), gathered(small), gathered(out)),
+        in_specs=[pl.BlockSpec(memory_space=pltpu.SMEM)] + [held] * 4,
+        out_specs=(held,) * 4,
         scratch_shapes=[
             pltpu.VMEM(pieces.shape, pieces.dtype),
             pltpu.VMEM(pieces.shape, pieces.dtype),
-            pltpu.SemaphoreType.DMA((6,)),
-            pltpu.SemaphoreType.DMA((4, groups)),
-            pltpu.SemaphoreType.DMA((4, groups)),
-            pltpu.SemaphoreType.DMA((6, groups, 1 + inner)),
-            pltpu.SemaphoreType.DMA((6, groups)),
+            pltpu.SemaphoreType.DMA((CHUNKS + 4,)),
+            pltpu.SemaphoreType.DMA((3, groups)),
+            pltpu.SemaphoreType.DMA((3, groups)),
+            pltpu.SemaphoreType.DMA((CHUNKS + 1, groups, 1 + inner)),
+            pltpu.SemaphoreType.DMA((CHUNKS + 1, groups)),
         ],
         compiler_params=pltpu.CompilerParams(collective_id=0, has_side_effects=True),
         cost_estimate=pl.CostEstimate(
             flops=0, bytes_accessed=4 * groups * out.size, transcendentals=0
         ),
-    )(extra_from, pieces, conv, small, ssm, out)
+    )(extra_from, pieces, conv, small, out)
 
 
 def mix_kernel(rows_ref, weight_ref, out_ref):
@@ -433,16 +440,15 @@
     coef_width = coef_proj.shape[1]
     coef_depth = -(-coef_width // 16) * 16
     small = jnp.concatenate([padded(coef_proj.T, coef_depth), delta_proj], axis=0)
-    extra, conv_base, small, ssm_base, out_whole = move(
+    ssm_base = lax.all_to_all(ssm_base, "dp", split_axis=0, concat_axis=0, tiled=True)
+    extra, conv_base, small, out_whole = move(
         extra_from,
         pieces,
         conv_blocks,
         small,
-        ssm_base.reshape(groups, ssm_rows, channels),
         out_proj,
     )
     extra = extra.reshape(groups * depth, channels)
-    ssm_base = ssm_base.reshape(row_count, state_len, channels)
     ssm_extra = extra[:ssm_rows].reshape(cap, state_len, channels)
     conv_extra = extra[ssm_rows : ssm_rows + conv_rows].reshape(cap, taps_kept, channels)
     conv_base = conv_base[:, :conv_rows].reshape(row_count, taps_kept, channels)
@@ -479,18 +485,30 @@
     ).reshape(steps_total, row_count, channels)
     step_size = jnp.where(active.T[:, :, None], step_size, 0.0)
 
-    mixed, ssm_final = scan(
-        slot,
-        ssm_base,
-        ssm_extra,
-        step_size,
-        activated,
-        gate_steps,
-        coef,
-        active.astype(jnp.int32),
-        -jnp.exp(decay_log),
-        skip_gain[None],
-    )
+    decay_rate = -jnp.exp(decay_log)
+    parts = 2
+    layer_parts, final_parts = [], []
+    for part in range(parts):
+        mixed, final = scan(
+            part,
+            parts,
+            slot,
+            ssm_base,
+            ssm_extra,
+            step_size,
+            activated,
+            gate_steps,
+            coef,
+            active.astype(jnp.int32),
+            decay_rate,
+            skip_gain[None],
+        )
+        partial_mix = mix(mixed.reshape(-1, channels), out_whole)
+        summed = lax.psum_scatter(partial_mix, "mp", scatter_dimension=1, tiled=True)
+        layer_parts.append(summed.reshape(steps_total, row_count // parts, -1))
+        final_parts.append(final)
+    layer_out = jnp.concatenate(layer_parts, axis=1)
+    ssm_final = jnp.concatenate(final_parts, axis=0)
     last = jnp.minimum(remain_new, steps_total)[:, None]
     window = []
     for k in range(taps_kept):
@@ -499,12 +517,6 @@
             entry = jnp.where(last == t, sequence[k + t], entry)
         window.append(entry)
     conv_final = jnp.stack(window, axis=1)
-
-    partial_mix = mix(mixed.reshape(steps_total * row_count, channels), out_whole)
-    summed = lax.psum_scatter(
-        partial_mix, "mp", scatter_dimension=1, tiled=True
-    )
-    layer_out = summed.reshape(steps_total, row_count, summed.shape[1])
     return (layer_out, conv_final, ssm_final)
 
 

time: 650 us -> 580 us (0.89)
  Pallas kernels: 509 us -> 412 us
  waiting for transfers between devices: 61.3 us -> 78 us
  other arithmetic: 17 us -> 24.3 us
  starting transfers between devices: 0.3 us -> 7.59 us
    pallas_call x1, Pallas kernels: 457 us -> 349 us  [move(): pl.pallas_call(functools.partial(move_kernel, groups, inner), out_shape=(...]
    psum x1, waiting for transfers between devices: 26.4 us -> 56.6 us  [per_device(): low_rank = lax.psum(partial_value.astype(jnp.bfloat16), 'mp')]
    reduce_scatter x1 -> x2, waiting for transfers between devices: 34.9 us -> 21.4 us  [per_device(): lax.psum_scatter(partial_mix, 'mp', scatter_dimension=1, tiled=True)]
    pallas_call x1 -> x2, Pallas kernels: 12.9 us -> 20.8 us  [mix(): pl.pallas_call(mix_kernel, out_shape=jax.ShapeDtypeStruct((count, groups...]
    concatenate x0 -> x2, other arithmetic: none -> 7.27 us  [the longest x1 5.23 us: per_device(): ssm_final = jnp.concatenate(final_parts, axis=0)]
    all_to_all x0 -> x1, starting transfers between devices: none -> 7.25 us  [per_device(): lax.all_to_all(ssm_base, 'dp', split_axis=0, concat_axis=0, tiled=True)]
    pallas_call x1 -> x2, Pallas kernels: 31.1 us -> 35.7 us  [scan(): pl.pallas_call(functools.partial(scan_kernel, start), out_shape=(jax.Shap...]
  transfers between devices with their start and end apart: 2 -> 4, of which waited for: 2 -> 2; matrix products, arithmetic and copies ran while one was open for 1% -> 10% of each run, Pallas kernels for 0% -> 65%
where the time goes in v3:
time: 580 us; the launch traced here: 579 us
  Pallas kernels  412 us (71%)
  waiting for transfers between devices  78 us (13%)
  local copies, waits for them, and re-layouts  35.6 us (6%)
  other arithmetic  24.3 us (4%)
  between operations  14.3 us (2%)
  starting transfers between devices  7.59 us (1%)
  matrix products  6.43 us (1%)
    pallas_call x1, Pallas kernels, move(): pl.pallas_call(functools.partial(move_kernel, groups, inner), out_shape=(...  349 us
    psum x1, waiting for transfers between devices, per_device(): low_rank = lax.psum(partial_value.astype(jnp.bfloat16), 'mp')  56.6 us
    pallas_call x2, Pallas kernels, scan(): pl.pallas_call(functools.partial(scan_kernel, start), out_shape=(jax.Shap...  35.7 us
    reduce_scatter x2, waiting for transfers between devices, per_device(): lax.psum_scatter(partial_mix, 'mp', scatter_dimension=1, tiled=True)  21.4 us
    pallas_call x2, Pallas kernels, mix(): pl.pallas_call(mix_kernel, out_shape=jax.ShapeDtypeStruct((count, groups...  20.8 us
  transfers between devices with their start and end apart: 4, of which 2 were waited for; matrix products, arithmetic and copies ran while one was open for 10% of the time, Pallas kernels for 65%

profile of v3, /device:TPU:0, one launch (start us, length us, event | category | flops | bytes accessed | tf_op | source)
XLA Modules:
  0.0 578.7 jit_solution(5193324865707296509)
XLA Ops:
  8.5 7.4 %shard_map.157 = (bf16[96,16,2048]{2,1,0:T(8,128)(2,1)}, bf16[12,16,2048]{2,1,0:T(8,128)(2,1)S(1)}) custom-call(s32[108]{0:T(128)S(1)} %select_reduce_fusion.index_ref, bf16[96,16,2048]{2,1,0:T(8,128)(2,1)} %state_ref.1), custom_call_target="tpu_custom_call" | custom-call | bytes 12582912 | tf_op jit(solution)/shard_map/pallas_call | solution.py:30
  15.9 7.3 %all-to-all-start = ((bf16[96,16,2048]{2,1,0:T(8,128)(2,1)}), bf16[96,16,2048]{2,1,0:T(8,128)(2,1)}, u32[]{:S(2)}, u32[]{:S(2)}) async-start(bf16[96,16,2048]{2,1,0:T(8,128)(2,1)} %get-tuple-element.13), calls=%async_computation | async-start | bytes 12582912 | tf_op jit(solution)/shard_map/all_to_all | solution.py:443
  23.3 4.9 gather_fusion
  30.6 2.4 reshape.576
  33.0 2.7 pad.13.conv_ref
  38.3 348.7 %shard_map.158 = (bf16[8,32,2048]{2,1,0:T(8,128)(2,1)}, bf16[8,48,2048]{2,1,0:T(8,128)(2,1)}, bf16[8,144,2048]{2,1,0:T(8,128)(2,1)}, bf16[8,2048,512]{2,1,0:T(8,128)(2,1)}) custom-call(s32[8]{0:T(128)} %select_reduce_fusion.1.from_ref, bf16[8,32,2048]{2,1,0:T(8,128)(2,1)} %bitcast.79, bf16[8,48,2048]{2,1,0:T(8,128)(2,1)} %pad.13.conv_ref, ...), custom_call_target="tpu_custom_call" | custom-call | bytes 33554432 | tf_op jit(solution)/shard_map/pallas_call | solution.py:318
  389.4 2.1 reshape.578
  391.5 1.8 slice.89
  393.4 2.1 reshape.581
  395.7 3.7 pad_maximum_fusion.2
  399.5 3.4 gather_fusion.1
  402.9 1.7 fusion.34
  410.6 2.1 convolution_convert_fusion
  413.1 3.2 slice.91
  416.4 56.6 %all-reduce.5.cloned.1.call-done = bf16[384,544]{0,1:T(8,128)(2,1)} async-done(((bf16[384,544]{0,1:T(8,128)(2,1)}), bf16[384,544]{0,1:T(8,128)(2,1)}) %all-reduce.5.cloned.1.call-update) | async-done | bytes 417808 | tf_op jit(solution)/shard_map/psum | solution.py:477
  474.3 4.3 compare_select_fusion
  478.7 3.3 pad_maximum_fusion.1
  482.0 17.8 %shard_map.161 = (bf16[4,48,2048]{2,1,0:T(8,128)(2,1)S(1)}, bf16[48,16,2048]{2,1,0:T(8,128)(2,1)}) custom-call(s32[96]{0:T(128)S(1)} %get-tuple-element.24.slot_ref, bf16[96,16,2048]{2,1,0:T(8,128)(2,1)} %all-to-all-done.base_ref, bf16[12,16,2048]{2,1,0:T(8,128)(2,1)S(1)} %bitcast.72, f32[4,96,2048]{2,1,0:T(8,128)} %get-tuple-element.46.step_ref, ...), custom_call_target="tpu_custom_call" | custom-call | flops 50331648 | bytes 25165824 | tf_op jit(solution)/shard_map/pallas_call | solution.py:120
  499.8 9.8 %shard_map.162 = bf16[192,4096]{1,0:T(8,128)(2,1)S(1)} custom-call(bf16[192,2048]{1,0:T(8,128)(2,1)S(1)} %bitcast.75, bf16[8,2048,512]{2,1,0:T(8,128)(2,1)} %get-tuple-element.19.weight_ref), custom_call_target="tpu_custom_call" | custom-call | flops 3221225472 | bytes 16777216 | tf_op jit(solution)/shard_map/pallas_call | solution.py:348
  511.0 17.8 %shard_map.159 = (bf16[4,48,2048]{2,1,0:T(8,128)(2,1)S(1)}, bf16[48,16,2048]{2,1,0:T(8,128)(2,1)}) custom-call(s32[96]{0:T(128)S(1)} %get-tuple-element.24.slot_ref, bf16[96,16,2048]{2,1,0:T(8,128)(2,1)} %all-to-all-done.base_ref, bf16[12,16,2048]{2,1,0:T(8,128)(2,1)S(1)} %bitcast.73, f32[4,96,2048]{2,1,0:T(8,128)} %get-tuple-element.46.step_ref, ...), custom_call_target="tpu_custom_call" | custom-call | flops 50331648 | bytes 25165824 | tf_op jit(solution)/shard_map/pallas_call | solution.py:120
  528.8 10.9 %shard_map.160 = bf16[192,4096]{1,0:T(8,128)(2,1)} custom-call(bf16[192,2048]{1,0:T(8,128)(2,1)S(1)} %bitcast.74, bf16[8,2048,512]{2,1,0:T(8,128)(2,1)} %get-tuple-element.19.weight_ref), custom_call_target="tpu_custom_call" | custom-call | flops 3221225472 | bytes 16777216 | tf_op jit(solution)/shard_map/pallas_call | solution.py:348
  543.5 5.2 pad_maximum_fusion
  548.7 21.4 %reduce-scatter.3.cloned.1.call-done = bf16[192,1024]{1,0:T(8,128)(2,1)} async-done(((bf16[192,4096]{1,0:T(8,128)(2,1)}), bf16[192,1024]{1,0:T(8,128)(2,1)}) %reduce-scatter.3.cloned.1.call-update) | async-done | bytes 393232 | tf_op jit(solution)/shard_map/reduce_scatter | solution.py:507
  570.1 2.0 pad_maximum_fusion.4
  (117 shorter events, 21.6 us)
Async XLA Ops:
  7.2 16.1 %copy-start = (bf16[96,3,2048]{2,0,1:T(8,128)(2,1)S(1)}, bf16[96,3,2048]{2,0,1:T(8,128)(2,1)}, u32[]{:S(2)}) copy-start(bf16[96,3,2048]{2,0,1:T(8,128)(2,1)} %param.16) | copy-start | bytes 3538948
  15.9 466.1 %all-to-all-start = ((bf16[96,16,2048]{2,1,0:T(8,128)(2,1)}), bf16[96,16,2048]{2,1,0:T(8,128)(2,1)}, u32[]{:S(2)}, u32[]{:S(2)}) async-start(bf16[96,16,2048]{2,1,0:T(8,128)(2,1)} %get-tuple-element.13), calls=%async_computation | async-start | bytes 12582912 | tf_op jit(solution)/shard_map/all_to_all | solution.py:443
  23.2 449.8 %all-reduce.5.cloned.1.call-start = ((), (), s32[]{:S(2)}) async-start(), calls=%async_computation.3 | async-start | bytes 835584 | tf_op jit(solution)/shard_map/psum | solution.py:477
  33.0 3.4 copy-start.24
  33.0 3.4 copy-start.25
  33.0 4.2 copy-start.23
  393.4 2.1 copy-start.28
  399.5 3.4 copy-start.27
  407.8 2.7 copy-start.20
  410.6 2.4 copy-start.22
  412.7 136.0 %reduce-scatter.5.cloned.1.call-start = ((), (), s32[]{:S(2)}) async-start(), calls=%async_computation.5 | async-start | bytes 1966080 | tf_op jit(solution)/shard_map/reduce_scatter | solution.py:507
  413.1 3.3 copy-start.26
  413.1 61.2 %copy-start.31 = (f32[2048]{0:T(1024)S(1)}, f32[2048]{0:T(1024)}, u32[]{:S(2)}) copy-start(f32[2048]{0:T(1024)} %param.24) | copy-start | bytes 24580
  474.3 4.4 copy-start.8
  474.3 4.4 copy-start.10
  474.3 4.4 copy-start.12
  474.3 4.3 copy-start.14
  478.7 3.3 copy-start.2
  478.7 3.3 copy-start.4
  510.9 59.2 %reduce-scatter.3.cloned.1.call-start = ((), (), s32[]{:S(2)}) async-start(), calls=%async_computation.4 | async-start | bytes 1966080 | tf_op jit(solution)/shard_map/reduce_scatter | solution.py:507
  528.8 11.0 %copy-start.16 = (bf16[96,1,2048]{2,0,1:T(8,128)(2,1)S(1)}, bf16[96,1,2048]{2,0,1:T(8,128)(2,1)}, u32[]{:S(2)}) copy-start(bf16[96,1,2048]{2,0,1:T(8,128)(2,1)} %copy-done.15) | copy-start | bytes 1179652
  528.8 11.0 %copy-start.18 = (bf16[96,1,2048]{2,0,1:T(8,128)(2,1)S(1)}, bf16[96,1,2048]{2,0,1:T(8,128)(2,1)}, u32[]{:S(2)}) copy-start(bf16[96,1,2048]{2,0,1:T(8,128)(2,1)} %copy-done.17) | copy-start | bytes 1179652
  541.2 2.3 copy-start.19
  543.5 28.7 %copy-start.1 = (bf16[96,3,2048]{2,0,1:T(8,128)(2,1)S(1)}, bf16[96,3,2048]{2,0,1:T(8,128)(2,1)}, u32[]{:S(2)}) copy-start(bf16[96,3,2048]{2,0,1:T(8,128)(2,1)} %param.16) | copy-start | bytes 3538948
  (12 other events, 18.0 us)
Sparse Core Ops, SparseCore 0:
  412.8 60.1 all-reduce.4
  511.1 28.2 reduce-scatter.4
  541.9 28.1 reduce-scatter.2

commit v4 on v3

--- a/solution.py
+++ b/solution.py
@@ -163,30 +163,8 @@
     )
 
 
-def move_kernel(
-    groups,
-    inner,
-    from_ref,
-    piece_ref,
-    conv_ref,
-    small_ref,
-    out_ref,
-    piece_out,
-    conv_out,
-    small_all,
-    out_all,
-    held,
-    passed,
-    own_sem,
-    send_sem,
-    recv_sem,
-    gather_send,
-    gather_recv,
-):
+def greet(groups):
     me = lax.axis_index("dp")
-    outer = groups // inner
-    mine_z = me // inner
-    mine_x = me % inner
     barrier = pltpu.get_barrier_semaphore()
     for k in range(1, groups):
         pl.semaphore_signal(
@@ -197,6 +175,94 @@
         )
     pl.semaphore_wait(barrier, groups - 1)
 
+
+def gather_blocks(groups, inner, parts, own_sem, send_sem, recv_sem, between):
+    me = lax.axis_index("dp")
+    outer = groups // inner
+    mine_z = me // inner
+    mine_x = me % inner
+
+    def copy_of(kind, src, dst, origin, lane, peer):
+        return remote(
+            src, dst.at[origin], send_sem.at[kind, origin, lane], recv_sem.at[kind, origin], peer
+        )
+
+    def forward(kind, src, dst, origin, ups):
+        for up in ups:
+            peer = me + inner if up else me - inner
+            room = mine_z + 1 < outer if up else mine_z >= 1
+
+            @pl.when(room)
+            def _():
+                copy_of(kind, src, dst, origin, 0 if up else 1, peer).start()
+
+        for k in range(1, inner):
+            peer = mine_z * inner + (mine_x + k) % inner
+            copy_of(kind, src, dst, origin, 1 + k, peer).start()
+
+    def arrived(kind, dst, origin):
+        copy_of(kind, dst.at[origin], dst, origin, 0, me).wait_recv()
+
+    own = []
+    for kind, (src, dst) in enumerate(parts):
+        forward(kind, src, dst, me, (True, False))
+        copy = pltpu.make_async_copy(src, dst.at[me], own_sem.at[kind])
+        copy.start()
+        own.append(copy)
+    between()
+    for s in range(1, outer):
+        for kind, (_, dst) in enumerate(parts):
+            for up in (True, False):
+                origin = me - s * inner if up else me + s * inner
+                there = mine_z >= s if up else mine_z + s < outer
+
+                @pl.when(there)
+                def _():
+                    arrived(kind, dst, origin)
+                    forward(kind, dst.at[origin], dst, origin, (up,))
+
+    for kind, (src, dst) in enumerate(parts):
+        for z in range(outer):
+            for k in range(1, inner):
+                arrived(kind, dst, z * inner + (mine_x + k) % inner)
+        own[kind].wait()
+        for z in range(outer):
+            origin = z * inner + mine_x
+
+            @pl.when((mine_z >= z) & (mine_z + 1 < outer))
+            def _():
+                copy_of(kind, src, dst, origin, 0, me).wait_send()
+
+            @pl.when((mine_z <= z) & (mine_z >= 1))
+            def _():
+                copy_of(kind, src, dst, origin, 1, me).wait_send()
+
+            for k in range(1, inner):
+                copy_of(kind, src, dst, origin, 1 + k, me).wait_send()
+
+
+def move_kernel(
+    groups,
+    inner,
+    from_ref,
+    piece_ref,
+    conv_ref,
+    small_ref,
+    piece_out,
+    conv_out,
+    small_all,
+    held,
+    passed,
+    own_sem,
+    send_sem,
+    recv_sem,
+    gather_own,
+    gather_send,
+    gather_recv,
+):
+    me = lax.axis_index("dp")
+    greet(groups)
+
     def exchange(kind, src, dst):
         copies = []
         for k in range(1, groups):
@@ -206,7 +272,7 @@
             )
             copy.start()
             copies.append(copy)
-        own = pltpu.make_async_copy(src.at[me], dst.at[me], own_sem.at[CHUNKS + 1 + kind])
+        own = pltpu.make_async_copy(src.at[me], dst.at[me], own_sem.at[kind])
         own.start()
         return copies, own
 
@@ -216,124 +282,97 @@
             copy.wait_recv()
         own.wait()
 
-    def gather_copy(kind, src, dst, origin, lane, peer):
-        return remote(
-            src, dst.at[origin], gather_send.at[kind, origin, lane], gather_recv.at[kind, origin], peer
-        )
-
-    def across(kind, src, dst, origin):
-        for k in range(1, inner):
-            peer = mine_z * inner + (mine_x + k) % inner
-            gather_copy(kind, src, dst, origin, 1 + k, peer).start()
-
-    def along(kind, src, dst, origin, up):
-        peer = me + inner if up else me - inner
-        room = mine_z + 1 < outer if up else mine_z >= 1
-
-        @pl.when(room)
-        def _():
-            gather_copy(kind, src, dst, origin, 0 if up else 1, peer).start()
-
-    def gather_first(kind, src, dst):
-        along(kind, src, dst, me, True)
-        along(kind, src, dst, me, False)
-        across(kind, src, dst, me)
-        own = pltpu.make_async_copy(src, dst.at[me], own_sem.at[kind])
-        own.start()
-        return own
-
-    def arrived(kind, dst, origin):
-        gather_copy(kind, dst.at[origin], dst, origin, 0, me).wait_recv()
-
-    def gather_rest(kind, dst, s):
-        for up in (True, False):
-            origin = me - s * inner if up else me + s * inner
-            there = mine_z >= s if up else mine_z + s < outer
-
-            @pl.when(there)
-            def _():
-                arrived(kind, dst, origin)
-                along(kind, dst.at[origin], dst, origin, up)
-                across(kind, dst.at[origin], dst, origin)
-
-    def gather_end(kind, src, dst, own):
-        for z in range(outer):
-            for k in range(1, inner):
-                arrived(kind, dst, z * inner + (mine_x + k) % inner)
-        own.wait()
-        for z in range(outer):
-            origin = z * inner + mine_x
-
-            @pl.when((mine_z >= z) & (mine_z + 1 < outer))
-            def _():
-                gather_copy(kind, src, dst, origin, 0, me).wait_send()
-
-            @pl.when((mine_z <= z) & (mine_z >= 1))
-            def _():
-                gather_copy(kind, src, dst, origin, 1, me).wait_send()
-
-            for k in range(1, inner):
-                gather_copy(kind, src, dst, origin, 1 + k, me).wait_send()
-
     first = exchange(0, piece_ref, held)
     conv = exchange(1, conv_ref, conv_out)
-    small_own = gather_first(CHUNKS, small_ref, small_all)
-    depth = out_ref.shape[0] // CHUNKS
+    second = []
+
+    def pass_on():
+        finish(first)
+        for h in range(groups):
+            passed[h] = held[from_ref[h]]
+        second.append(exchange(2, passed, piece_out))
+
+    gather_blocks(
+        groups, inner, [(small_ref, small_all)], gather_own, gather_send, gather_recv, pass_on
+    )
+    finish(conv)
+    finish(second[0])
+    for copies, _ in (first, conv, second[0]):
+        for copy in copies:
+            copy.wait_send()
+
+
+def gather_kernel(groups, inner, src_ref, all_ref, own_sem, send_sem, recv_sem):
+    greet(groups)
+    depth = src_ref.shape[0] // CHUNKS
     parts = [
-        (c, out_ref.at[pl.ds(c * depth, depth)], out_all.at[:, pl.ds(c * depth, depth)])
+        (src_ref.at[pl.ds(c * depth, depth)], all_ref.at[:, pl.ds(c * depth, depth)])
         for c in range(CHUNKS)
     ]
-    out_own = [gather_first(*part) for part in parts]
-    finish(first)
-    for h in range(groups):
-        passed[h] = held[from_ref[h]]
-    second = exchange(2, passed, piece_out)
-    for s in range(1, outer):
-        gather_rest(CHUNKS, small_all, s)
-        for c, _, whole in parts:
-            gather_rest(c, whole, s)
-    gather_end(CHUNKS, small_ref, small_all, small_own)
-    finish(conv)
-    finish(second)
-    for (c, part, whole), own in zip(parts, out_own):
-        gather_end(c, part, whole, own)
-    for copies, _ in (first, conv, second):
-        for copy in copies:
-            copy.wait_send()
-
-
-def move(extra_from, pieces, conv, small, out):
-    groups = pieces.shape[0]
+    gather_blocks(groups, inner, parts, own_sem, send_sem, recv_sem, lambda: None)
+
+
+def inner_of(groups):
     inner = 1
     while inner * inner * 4 <= groups:
         inner *= 2
+    return inner
+
+
+def gather_scratch(kinds, groups, inner):
+    return [
+        pltpu.SemaphoreType.DMA((kinds,)),
+        pltpu.SemaphoreType.DMA((kinds, groups, 1 + inner)),
+        pltpu.SemaphoreType.DMA((kinds, groups)),
+    ]
+
+
+def move(extra_from, pieces, conv, small):
+    groups = pieces.shape[0]
+    inner = inner_of(groups)
     held = pl.BlockSpec(memory_space=pl.ANY)
 
     def like(array):
         return jax.ShapeDtypeStruct(array.shape, array.dtype)
 
-    def gathered(array):
-        return jax.ShapeDtypeStruct((groups,) + array.shape, array.dtype)
-
     return pl.pallas_call(
         functools.partial(move_kernel, groups, inner),
-        out_shape=(like(pieces), like(conv), gathered(small), gathered(out)),
-        in_specs=[pl.BlockSpec(memory_space=pltpu.SMEM)] + [held] * 4,
-        out_specs=(held,) * 4,
+        out_shape=(
+            like(pieces),
+            like(conv),
+            jax.ShapeDtypeStruct((groups,) + small.shape, small.dtype),
+        ),
+        in_specs=[pl.BlockSpec(memory_space=pltpu.SMEM)] + [held] * 3,
+        out_specs=(held,) * 3,
         scratch_shapes=[
             pltpu.VMEM(pieces.shape, pieces.dtype),
             pltpu.VMEM(pieces.shape, pieces.dtype),
-            pltpu.SemaphoreType.DMA((CHUNKS + 4,)),
+            pltpu.SemaphoreType.DMA((3,)),
             pltpu.SemaphoreType.DMA((3, groups)),
             pltpu.SemaphoreType.DMA((3, groups)),
-            pltpu.SemaphoreType.DMA((CHUNKS + 1, groups, 1 + inner)),
-            pltpu.SemaphoreType.DMA((CHUNKS + 1, groups)),
-        ],
+        ]
+        + gather_scratch(1, groups, inner),
         compiler_params=pltpu.CompilerParams(collective_id=0, has_side_effects=True),
         cost_estimate=pl.CostEstimate(
-            flops=0, bytes_accessed=4 * groups * out.size, transcendentals=0
-        ),
-    )(extra_from, pieces, conv, small, out)
+            flops=0, bytes_accessed=64 * groups * small.size, transcendentals=0
+        ),
+    )(extra_from, pieces, conv, small)
+
+
+def gather(block, groups):
+    inner = inner_of(groups)
+    held = pl.BlockSpec(memory_space=pl.ANY)
+    return pl.pallas_call(
+        functools.partial(gather_kernel, groups, inner),
+        out_shape=jax.ShapeDtypeStruct((groups,) + block.shape, block.dtype),
+        in_specs=[held],
+        out_specs=held,
+        scratch_shapes=gather_scratch(CHUNKS, groups, inner),
+        compiler_params=pltpu.CompilerParams(collective_id=1, has_side_effects=True),
+        cost_estimate=pl.CostEstimate(
+            flops=0, bytes_accessed=32 * groups * block.size, transcendentals=0
+        ),
+    )(block)
 
 
 def mix_kernel(rows_ref, weight_ref, out_ref):
@@ -441,12 +480,11 @@
     coef_depth = -(-coef_width // 16) * 16
     small = jnp.concatenate([padded(coef_proj.T, coef_depth), delta_proj], axis=0)
     ssm_base = lax.all_to_all(ssm_base, "dp", split_axis=0, concat_axis=0, tiled=True)
-    extra, conv_base, small, out_whole = move(
+    extra, conv_base, small = move(
         extra_from,
         pieces,
         conv_blocks,
         small,
-        out_proj,
     )
     extra = extra.reshape(groups * depth, channels)
     ssm_extra = extra[:ssm_rows].reshape(cap, state_len, channels)
@@ -474,7 +512,11 @@
         (((1,), (1,)), ((), ())),
         preferred_element_type=jnp.float32,
     )
-    low_rank = lax.psum(partial_value.astype(jnp.bfloat16), "mp")
+    partial_value, out_proj = lax.optimization_barrier(
+        (partial_value.astype(jnp.bfloat16), out_proj)
+    )
+    out_whole = gather(out_proj, groups)
+    low_rank = lax.psum(partial_value, "mp")
     coef = low_rank[:, rank_len:].astype(jnp.float32)
     coef = coef.reshape(steps_total, row_count, 2, state_len)
     coef = coef.transpose(1, 3, 0, 2).reshape(row_count, state_len, 2 * steps_total)

time: 580 us -> 615 us (1.060)
  Pallas kernels: 412 us -> 506 us
  waiting for transfers between devices: 78 us -> 19.6 us
    pallas_call x0 -> x1, Pallas kernels: none -> 187 us  [gather(): pl.pallas_call(functools.partial(gather_kernel, groups, inner), out_shape...]
    pallas_call x1, Pallas kernels: 349 us -> 255 us  [move(): pl.pallas_call(functools.partial(move_kernel, groups, inner), out_shape=(...]
    psum x1, waiting for transfers between devices: 56.6 us -> 0.02 us  [per_device(): low_rank = lax.psum(partial_value, 'mp')]
  transfers between devices with their start and end apart: 4 -> 4, of which waited for: 2 -> 1; matrix products, arithmetic and copies ran while one was open for 10% -> 9% of each run, Pallas kernels for 65% -> 77%
where the time goes in v4:
time: 615 us; the launch traced here: 614 us
  Pallas kernels  506 us (82%)
  local copies, waits for them, and re-layouts  35.7 us (6%)
  other arithmetic  24.4 us (4%)
  waiting for transfers between devices  19.6 us (3%)
  between operations  14.3 us (2%)
  starting transfers between devices  7.59 us (1%)
  matrix products  6.43 us (1%)
    pallas_call x1, Pallas kernels, move(): pl.pallas_call(functools.partial(move_kernel, groups, inner), out_shape=(...  255 us
    pallas_call x1, Pallas kernels, gather(): pl.pallas_call(functools.partial(gather_kernel, groups, inner), out_shape...  187 us
    pallas_call x2, Pallas kernels, scan(): pl.pallas_call(functools.partial(scan_kernel, start), out_shape=(jax.Shap...  35.7 us
    pallas_call x2, Pallas kernels, mix(): pl.pallas_call(mix_kernel, out_shape=jax.ShapeDtypeStruct((count, groups...  20.7 us
    reduce_scatter x2, waiting for transfers between devices, per_device(): lax.psum_scatter(partial_mix, 'mp', scatter_dimension=1, tiled=True)  19.5 us
  transfers between devices with their start and end apart: 4, of which 1 were waited for; matrix products, arithmetic and copies ran while one was open for 9% of the time, Pallas kernels for 77%

profile of v4, /device:TPU:0, one launch (start us, length us, event | category | flops | bytes accessed | tf_op | source)
XLA Modules:
  0.0 613.8 jit_solution(11725522143885716466)
XLA Ops:
  8.5 7.4 %shard_map.157 = (bf16[96,16,2048]{2,1,0:T(8,128)(2,1)}, bf16[12,16,2048]{2,1,0:T(8,128)(2,1)S(1)}) custom-call(s32[108]{0:T(128)S(1)} %select_reduce_fusion.index_ref, bf16[96,16,2048]{2,1,0:T(8,128)(2,1)} %state_ref.1), custom_call_target="tpu_custom_call" | custom-call | bytes 12582912 | tf_op jit(solution)/shard_map/pallas_call | solution.py:30
  15.9 7.3 %all-to-all-start = ((bf16[96,16,2048]{2,1,0:T(8,128)(2,1)}), bf16[96,16,2048]{2,1,0:T(8,128)(2,1)}, u32[]{:S(2)}, u32[]{:S(2)}) async-start(bf16[96,16,2048]{2,1,0:T(8,128)(2,1)} %get-tuple-element.14), calls=%async_computation | async-start | bytes 12582912 | tf_op jit(solution)/shard_map/all_to_all | solution.py:482
  23.3 4.9 gather_fusion
  30.2 2.4 reshape.576
  32.8 2.8 pad.13.conv_ref
  38.2 255.4 %shard_map.158 = (bf16[8,32,2048]{2,1,0:T(8,128)(2,1)}, bf16[8,48,2048]{2,1,0:T(8,128)(2,1)}, bf16[8,144,2048]{2,1,0:T(8,128)(2,1)}) custom-call(s32[8]{0:T(128)} %select_reduce_fusion.1.from_ref, bf16[8,32,2048]{2,1,0:T(8,128)(2,1)} %bitcast.79, bf16[8,48,2048]{2,1,0:T(8,128)(2,1)} %pad.13.conv_ref, bf16[144,2048]{1,0:T(8,128)(2,1)} %fusion.20.small_ref), custom_call_target="tpu_custom_call" | custom-call | bytes 150994944 | tf_op jit(solution)/shard_map/pallas_call | solution.py:338
  296.0 2.1 reshape.578
  298.3 1.8 slice.89
  300.2 2.1 reshape.581
  302.5 3.8 pad_maximum_fusion.2
  306.3 3.4 gather_fusion.1
  309.8 1.7 fusion.34
  317.4 2.1 convolution_convert_fusion
  319.9 3.3 slice.91
  323.2 186.7 %shard_map.160.weight_ref = bf16[8,2048,512]{2,1,0:T(8,128)(2,1)} custom-call(bf16[2048,512]{1,0:T(8,128)(2,1)} %src_ref), custom_call_target="tpu_custom_call" | custom-call | bytes 268435456 | tf_op jit(solution)/shard_map/pallas_call | solution.py:365
  511.4 4.3 compare_select_fusion
  515.8 3.3 pad_maximum_fusion.1
  519.0 17.8 %shard_map.159 = (bf16[4,48,2048]{2,1,0:T(8,128)(2,1)S(1)}, bf16[48,16,2048]{2,1,0:T(8,128)(2,1)}) custom-call(s32[96]{0:T(128)S(1)} %get-tuple-element.26.slot_ref, bf16[96,16,2048]{2,1,0:T(8,128)(2,1)} %all-to-all-done.base_ref, bf16[12,16,2048]{2,1,0:T(8,128)(2,1)S(1)} %bitcast.72, f32[4,96,2048]{2,1,0:T(8,128)} %get-tuple-element.48.step_ref, ...), custom_call_target="tpu_custom_call" | custom-call | flops 50331648 | bytes 25165824 | tf_op jit(solution)/shard_map/pallas_call | solution.py:120
  536.9 9.8 %shard_map.161 = bf16[192,4096]{1,0:T(8,128)(2,1)S(1)} custom-call(bf16[192,2048]{1,0:T(8,128)(2,1)S(1)} %bitcast.75, bf16[8,2048,512]{2,1,0:T(8,128)(2,1)} %shard_map.160.weight_ref), custom_call_target="tpu_custom_call" | custom-call | flops 3221225472 | bytes 16777216 | tf_op jit(solution)/shard_map/pallas_call | solution.py:387
  547.9 17.9 %shard_map.162 = (bf16[4,48,2048]{2,1,0:T(8,128)(2,1)S(1)}, bf16[48,16,2048]{2,1,0:T(8,128)(2,1)}) custom-call(s32[96]{0:T(128)S(1)} %get-tuple-element.26.slot_ref, bf16[96,16,2048]{2,1,0:T(8,128)(2,1)} %all-to-all-done.base_ref, bf16[12,16,2048]{2,1,0:T(8,128)(2,1)S(1)} %bitcast.73, f32[4,96,2048]{2,1,0:T(8,128)} %get-tuple-element.48.step_ref, ...), custom_call_target="tpu_custom_call" | custom-call | flops 50331648 | bytes 25165824 | tf_op jit(solution)/shard_map/pallas_call | solution.py:120
  565.8 10.9 %shard_map.163 = bf16[192,4096]{1,0:T(8,128)(2,1)} custom-call(bf16[192,2048]{1,0:T(8,128)(2,1)S(1)} %bitcast.74, bf16[8,2048,512]{2,1,0:T(8,128)(2,1)} %shard_map.160.weight_ref), custom_call_target="tpu_custom_call" | custom-call | flops 3221225472 | bytes 16777216 | tf_op jit(solution)/shard_map/pallas_call | solution.py:387
  580.5 5.3 pad_maximum_fusion
  585.7 19.5 %reduce-scatter.5.cloned.1.call-done = bf16[192,1024]{1,0:T(8,128)(2,1)} async-done(((bf16[192,4096]{1,0:T(8,128)(2,1)}), bf16[192,1024]{1,0:T(8,128)(2,1)}) %reduce-scatter.5.cloned.1.call-update) | async-done | bytes 393232 | tf_op jit(solution)/shard_map/reduce_scatter | solution.py:549
  605.2 2.0 pad_maximum_fusion.4
  (118 shorter events, 21.6 us)
Async XLA Ops:
  7.2 16.1 %copy-start = (bf16[96,3,2048]{2,0,1:T(8,128)(2,1)S(1)}, bf16[96,3,2048]{2,0,1:T(8,128)(2,1)}, u32[]{:S(2)}) copy-start(bf16[96,3,2048]{2,0,1:T(8,128)(2,1)} %param.16) | copy-start | bytes 3538948
  15.9 503.1 %all-to-all-start = ((bf16[96,16,2048]{2,1,0:T(8,128)(2,1)}), bf16[96,16,2048]{2,1,0:T(8,128)(2,1)}, u32[]{:S(2)}, u32[]{:S(2)}) async-start(bf16[96,16,2048]{2,1,0:T(8,128)(2,1)} %get-tuple-element.14), calls=%async_computation | async-start | bytes 12582912 | tf_op jit(solution)/shard_map/all_to_all | solution.py:482
  23.2 486.9 %all-reduce.5.cloned.1.call-start = ((), (), s32[]{:S(2)}) async-start(), calls=%async_computation.3 | async-start | bytes 835584 | tf_op jit(solution)/shard_map/psum | solution.py:519
  32.6 3.6 copy-start.24
  32.6 3.6 copy-start.25
  32.8 4.2 copy-start.23
  300.1 2.1 copy-start.28
  306.3 3.4 copy-start.27
  314.7 2.7 copy-start.20
  319.6 3.6 copy-start.22
  319.6 266.2 %reduce-scatter.3.cloned.1.call-start = ((), (), s32[]{:S(2)}) async-start(), calls=%async_computation.4 | async-start | bytes 1966080 | tf_op jit(solution)/shard_map/reduce_scatter | solution.py:549
  323.2 186.8 %copy-start.26 = (f32[16,2048]{1,0:T(8,128)S(1)}, f32[16,2048]{1,0:T(8,128)}, u32[]{:S(2)}) copy-start(f32[16,2048]{1,0:T(8,128)} %param.25) | copy-start | bytes 393220
  323.2 188.1 %copy-start.31 = (f32[2048]{0:T(1024)S(1)}, f32[2048]{0:T(1024)}, u32[]{:S(2)}) copy-start(f32[2048]{0:T(1024)} %param.24) | copy-start | bytes 24580
  511.3 4.4 copy-start.8
  511.4 4.4 copy-start.10
  511.4 4.4 copy-start.12
  511.4 4.3 copy-start.14
  515.7 3.3 copy-start.2
  515.7 3.3 copy-start.4
  547.9 57.3 %reduce-scatter.5.cloned.1.call-start = ((), (), s32[]{:S(2)}) async-start(), calls=%async_computation.5 | async-start | bytes 1966080 | tf_op jit(solution)/shard_map/reduce_scatter | solution.py:549
  565.8 10.9 %copy-start.16 = (bf16[96,1,2048]{2,0,1:T(8,128)(2,1)S(1)}, bf16[96,1,2048]{2,0,1:T(8,128)(2,1)}, u32[]{:S(2)}) copy-start(bf16[96,1,2048]{2,0,1:T(8,128)(2,1)} %copy-done.15) | copy-start | bytes 1179652
  565.8 10.9 %copy-start.18 = (bf16[96,1,2048]{2,0,1:T(8,128)(2,1)S(1)}, bf16[96,1,2048]{2,0,1:T(8,128)(2,1)}, u32[]{:S(2)}) copy-start(bf16[96,1,2048]{2,0,1:T(8,128)(2,1)} %copy-done.17) | copy-start | bytes 1179652
  578.1 2.3 copy-start.19
  580.5 26.8 %copy-start.1 = (bf16[96,3,2048]{2,0,1:T(8,128)(2,1)S(1)}, bf16[96,3,2048]{2,0,1:T(8,128)(2,1)}, u32[]{:S(2)}) copy-start(bf16[96,3,2048]{2,0,1:T(8,128)(2,1)} %param.16) | copy-start | bytes 3538948
  (12 other events, 18.0 us)
Sparse Core Ops, SparseCore 0:
  319.7 34.5 all-reduce.4
  548.0 26.4 reduce-scatter.2
  577.0 28.1 reduce-scatter.4

commit v5 on v4

--- a/solution.py
+++ b/solution.py
@@ -479,13 +479,14 @@
     coef_width = coef_proj.shape[1]
     coef_depth = -(-coef_width // 16) * 16
     small = jnp.concatenate([padded(coef_proj.T, coef_depth), delta_proj], axis=0)
-    ssm_base = lax.all_to_all(ssm_base, "dp", split_axis=0, concat_axis=0, tiled=True)
     extra, conv_base, small = move(
         extra_from,
         pieces,
         conv_blocks,
         small,
     )
+    ssm_base, extra = lax.optimization_barrier((ssm_base, extra))
+    ssm_base = lax.all_to_all(ssm_base, "dp", split_axis=0, concat_axis=0, tiled=True)
     extra = extra.reshape(groups * depth, channels)
     ssm_extra = extra[:ssm_rows].reshape(cap, state_len, channels)
     conv_extra = extra[ssm_rows : ssm_rows + conv_rows].reshape(cap, taps_kept, channels)

time: 615 us -> 569 us (0.925)
  Pallas kernels: 506 us -> 428 us
  waiting for transfers between devices: 19.6 us -> 54.1 us
    pallas_call x1, Pallas kernels: 255 us -> 141 us  [move(): pl.pallas_call(functools.partial(move_kernel, groups, inner), out_shape=(...]
    pallas_call x1, Pallas kernels: 187 us -> 223 us  [gather(): pl.pallas_call(functools.partial(gather_kernel, groups, inner), out_shape...]
    reduce_scatter x2, waiting for transfers between devices: 19.5 us -> 54 us  [per_device(): lax.psum_scatter(partial_mix, 'mp', scatter_dimension=1, tiled=True)]
  transfers between devices with their start and end apart: 4 -> 4, of which waited for: 1 -> 2; matrix products, arithmetic and copies ran while one was open for 9% -> 7% of each run, Pallas kernels for 77% -> 44%
where the time goes in v5:
time: 569 us; the launch traced here: 568 us
  Pallas kernels  428 us (75%)
  waiting for transfers between devices  54.1 us (10%)
  local copies, waits for them, and re-layouts  35.9 us (6%)
  other arithmetic  24.4 us (4%)
  between operations  14.3 us (3%)
  matrix products  6.43 us (1%)
    pallas_call x1, Pallas kernels, gather(): pl.pallas_call(functools.partial(gather_kernel, groups, inner), out_shape...  223 us
    pallas_call x1, Pallas kernels, move(): pl.pallas_call(functools.partial(move_kernel, groups, inner), out_shape=(...  141 us
    reduce_scatter x2, waiting for transfers between devices, per_device(): lax.psum_scatter(partial_mix, 'mp', scatter_dimension=1, tiled=True)  54 us
    pallas_call x2, Pallas kernels, scan(): pl.pallas_call(functools.partial(scan_kernel, start), out_shape=(jax.Shap...  35.7 us
    pallas_call x2, Pallas kernels, mix(): pl.pallas_call(mix_kernel, out_shape=jax.ShapeDtypeStruct((count, groups...  20.7 us
  transfers between devices with their start and end apart: 4, of which 2 were waited for; matrix products, arithmetic and copies ran while one was open for 7% of the time, Pallas kernels for 44%

profile of v5, /device:TPU:0, one launch (start us, length us, event | category | flops | bytes accessed | tf_op | source)
XLA Modules:
  0.0 568.3 jit_solution(6734870261632873697)
XLA Ops:
  8.6 4.9 gather_fusion
  14.6 7.4 %shard_map.157 = (bf16[96,16,2048]{2,1,0:T(8,128)(2,1)}, bf16[12,16,2048]{2,1,0:T(8,128)(2,1)S(1)}) custom-call(s32[108]{0:T(128)S(1)} %select_reduce_fusion.index_ref, bf16[96,16,2048]{2,1,0:T(8,128)(2,1)} %state_ref.1), custom_call_target="tpu_custom_call" | custom-call | bytes 12582912 | tf_op jit(solution)/shard_map/pallas_call | solution.py:30
  22.3 2.3 copy.28
  24.5 2.2 reshape.576
  31.1 141.2 %shard_map.158 = (bf16[8,32,2048]{2,1,0:T(8,128)(2,1)}, bf16[8,48,2048]{2,1,0:T(8,128)(2,1)}, bf16[8,144,2048]{2,1,0:T(8,128)(2,1)}) custom-call(s32[8]{0:T(128)} %select_reduce_fusion.1.from_ref, bf16[8,32,2048]{2,1,0:T(8,128)(2,1)} %bitcast.79, bf16[8,48,2048]{2,1,0:T(8,128)(2,1)} %pad.13.conv_ref, bf16[144,2048]{1,0:T(8,128)(2,1)} %fusion.20.small_ref), custom_call_target="tpu_custom_call" | custom-call | bytes 150994944 | tf_op jit(solution)/shard_map/pallas_call | solution.py:338
  172.3 4.8 all-to-all-start
  179.8 2.1 reshape.578
  182.1 1.8 slice.89
  183.9 2.1 reshape.581
  186.2 3.8 pad_maximum_fusion.2
  190.1 3.4 gather_fusion.1
  201.2 2.1 convolution_convert_fusion
  203.6 3.3 slice.91
  207.0 223.0 %shard_map.160.weight_ref = bf16[8,2048,512]{2,1,0:T(8,128)(2,1)} custom-call(bf16[2048,512]{1,0:T(8,128)(2,1)} %src_ref), custom_call_target="tpu_custom_call" | custom-call | bytes 268435456 | tf_op jit(solution)/shard_map/pallas_call | solution.py:365
  431.5 4.3 compare_select_fusion
  435.8 3.3 pad_maximum_fusion.1
  439.1 17.8 %shard_map.159 = (bf16[4,48,2048]{2,1,0:T(8,128)(2,1)S(1)}, bf16[48,16,2048]{2,1,0:T(8,128)(2,1)}) custom-call(s32[96]{0:T(128)S(1)} %get-tuple-element.30.slot_ref, bf16[96,16,2048]{2,1,0:T(8,128)(2,1)} %all-to-all-done.base_ref, bf16[12,16,2048]{2,1,0:T(8,128)(2,1)S(1)} %bitcast.72, f32[4,96,2048]{2,1,0:T(8,128)} %get-tuple-element.52.step_ref, ...), custom_call_target="tpu_custom_call" | custom-call | flops 50331648 | bytes 25165824 | tf_op jit(solution)/shard_map/pallas_call | solution.py:120
  456.9 9.8 %shard_map.161 = bf16[192,4096]{1,0:T(8,128)(2,1)S(1)} custom-call(bf16[192,2048]{1,0:T(8,128)(2,1)S(1)} %bitcast.75, bf16[8,2048,512]{2,1,0:T(8,128)(2,1)} %shard_map.160.weight_ref), custom_call_target="tpu_custom_call" | custom-call | flops 3221225472 | bytes 16777216 | tf_op jit(solution)/shard_map/pallas_call | solution.py:387
  468.0 17.9 %shard_map.162 = (bf16[4,48,2048]{2,1,0:T(8,128)(2,1)S(1)}, bf16[48,16,2048]{2,1,0:T(8,128)(2,1)}) custom-call(s32[96]{0:T(128)S(1)} %get-tuple-element.30.slot_ref, bf16[96,16,2048]{2,1,0:T(8,128)(2,1)} %all-to-all-done.base_ref, bf16[12,16,2048]{2,1,0:T(8,128)(2,1)S(1)} %bitcast.73, f32[4,96,2048]{2,1,0:T(8,128)} %get-tuple-element.52.step_ref, ...), custom_call_target="tpu_custom_call" | custom-call | flops 50331648 | bytes 25165824 | tf_op jit(solution)/shard_map/pallas_call | solution.py:120
  485.9 10.8 %shard_map.163 = bf16[192,4096]{1,0:T(8,128)(2,1)} custom-call(bf16[192,2048]{1,0:T(8,128)(2,1)S(1)} %bitcast.74, bf16[8,2048,512]{2,1,0:T(8,128)(2,1)} %shard_map.160.weight_ref), custom_call_target="tpu_custom_call" | custom-call | flops 3221225472 | bytes 16777216 | tf_op jit(solution)/shard_map/pallas_call | solution.py:387
  500.5 5.2 pad_maximum_fusion
  505.7 23.2 %reduce-scatter.3.cloned.1.call-done = bf16[192,1024]{1,0:T(8,128)(2,1)} async-done(((bf16[192,4096]{1,0:T(8,128)(2,1)}), bf16[192,1024]{1,0:T(8,128)(2,1)}) %reduce-scatter.3.cloned.1.call-update) | async-done | bytes 393232 | tf_op jit(solution)/shard_map/reduce_scatter | solution.py:550
  529.0 30.8 %reduce-scatter.5.cloned.1.call-done = bf16[192,1024]{1,0:T(8,128)(2,1)} async-done(((bf16[192,4096]{1,0:T(8,128)(2,1)}), bf16[192,1024]{1,0:T(8,128)(2,1)}) %reduce-scatter.5.cloned.1.call-update) | async-done | bytes 393232 | tf_op jit(solution)/shard_map/reduce_scatter | solution.py:550
  559.7 2.0 pad_maximum_fusion.4
  (118 shorter events, 24.4 us)
Async XLA Ops:
  28.3 1.9 copy-start.24
  28.3 1.9 copy-start.25
  172.3 266.8 %all-to-all-start = ((bf16[96,16,2048]{2,1,0:T(8,128)(2,1)}), bf16[96,16,2048]{2,1,0:T(8,128)(2,1)}, u32[]{:S(2)}, u32[]{:S(2)}) async-start(bf16[96,16,2048]{2,1,0:T(8,128)(2,1)} %get-tuple-element.19), calls=%async_computation | async-start | bytes 12582912 | tf_op jit(solution)/shard_map/all_to_all | solution.py:489
  177.1 253.0 %all-reduce.5.cloned.1.call-start = ((), (), s32[]{:S(2)}) async-start(), calls=%async_computation.3 | async-start | bytes 835584 | tf_op jit(solution)/shard_map/psum | solution.py:520
  183.9 2.1 copy-start.28
  183.9 2.1 copy-start.30
  190.1 3.4 copy-start.27
  198.4 2.7 copy-start.21
  203.3 3.6 copy-start.23
  203.3 325.6 %reduce-scatter.3.cloned.1.call-start = ((), (), s32[]{:S(2)}) async-start(), calls=%async_computation.4 | async-start | bytes 1966080 | tf_op jit(solution)/shard_map/reduce_scatter | solution.py:550
  206.9 223.1 %copy-start.26 = (f32[16,2048]{1,0:T(8,128)S(1)}, f32[16,2048]{1,0:T(8,128)}, u32[]{:S(2)}) copy-start(f32[16,2048]{1,0:T(8,128)} %param.25) | copy-start | bytes 393220
  206.9 224.5 %copy-start.31 = (f32[2048]{0:T(1024)S(1)}, f32[2048]{0:T(1024)}, u32[]{:S(2)}) copy-start(f32[2048]{0:T(1024)} %param.24) | copy-start | bytes 24580
  431.4 4.4 copy-start.8
  431.4 4.4 copy-start.10
  431.4 4.4 copy-start.12
  431.4 4.3 copy-start.14
  435.8 3.3 copy-start.2
  435.8 3.3 copy-start.4
  468.0 91.8 %reduce-scatter.5.cloned.1.call-start = ((), (), s32[]{:S(2)}) async-start(), calls=%async_computation.5 | async-start | bytes 1966080 | tf_op jit(solution)/shard_map/reduce_scatter | solution.py:550
  485.9 10.9 %copy-start.17 = (bf16[96,1,2048]{2,0,1:T(8,128)(2,1)S(1)}, bf16[96,1,2048]{2,0,1:T(8,128)(2,1)}, u32[]{:S(2)}) copy-start(bf16[96,1,2048]{2,0,1:T(8,128)(2,1)} %copy-done.16) | copy-start | bytes 1179652
  485.9 10.9 %copy-start.19 = (bf16[96,1,2048]{2,0,1:T(8,128)(2,1)S(1)}, bf16[96,1,2048]{2,0,1:T(8,128)(2,1)}, u32[]{:S(2)}) copy-start(bf16[96,1,2048]{2,0,1:T(8,128)(2,1)} %copy-done.18) | copy-start | bytes 1179652
  496.7 1.8 copy-start.22
  498.1 2.3 copy-start.20
  500.5 61.3 %copy-start.1 = (bf16[96,3,2048]{2,0,1:T(8,128)(2,1)S(1)}, bf16[96,3,2048]{2,0,1:T(8,128)(2,1)}, u32[]{:S(2)}) copy-start(bf16[96,3,2048]{2,0,1:T(8,128)(2,1)} %param.16) | copy-start | bytes 3538948
  (12 other events, 17.1 us)
Sparse Core Ops, SparseCore 0:
  203.4 33.6 all-reduce.4
  468.1 60.8 reduce-scatter.2
  531.5 28.1 reduce-scatter.4
